TPU v7x, 256 devices: a whole 4x4x8 slice. The times are simulated.
256 devices in a mesh: chan: 32 (over y, x, core), band: 8 (over z).
Axes of the slice: x: 4, y: 4, z: 8, core: 2. Of those that a mesh axis runs over, the one named last changes fastest.
Arguments:
- spectra: bfloat16 [2, 30, 512, 8192], P(None, None, 'chan', 'band'), may hold values from -6 to 6
- source_block: int32 [1], replicated, may hold values from 0 to 127
- segment_flags: int32 [30], replicated, may hold values from 0 to 1, as said below
Outputs:
- correlations: float32 [64, 8, 1024, 1024], P(None, 'band', 'chan')
Inputs may be any that keep to these rules, and one draw needn't show every extreme that they name: `segment_flags`: at least one segment is valid.
All inputs are finite; a program needn't handle non-finite values.
Results may differ from a plain program's by a relative error of at most 0.0037.
Values may be sent and summed in bfloat16 or wider, within the bound.
A program may use at most 128 MiB of HBM per device.

v0:
```python
import math

import jax
import jax.numpy as jnp
from jax import lax
from jax.sharding import PartitionSpec as P

LAGS = 1024
F = 512
SRC = 64
RB = 1024


def spread(block, axis, owner):
    block = jnp.where(lax.axis_index(axis) == owner, block, jnp.zeros_like(block))
    return lax.psum(block, axis)


def lag_table():
    frequency = jnp.arange(F, dtype=jnp.int32)[:, None]
    shifted_lag = jnp.arange(LAGS, dtype=jnp.int32)[None, :] - LAGS // 2
    phase_index = frequency * shifted_lag % LAGS
    phase_angle = 2.0 * math.pi / LAGS * phase_index.astype(jnp.float32)
    weight = jnp.where(frequency == 0, 1.0, 2.0).astype(jnp.float32) / jnp.sqrt(jnp.float32(2 * F))
    cosine_component = weight * jnp.cos(phase_angle)
    sin_part = -weight * jnp.sin(phase_angle)
    return jnp.stack([cosine_component, sin_part], axis=1).astype(jnp.bfloat16)


def stack_segment_windows(source, receiver_traces, valid_mask, valid_window_count):
    masked = source * valid_mask[None, :, None, None]
    left_real = jnp.concatenate([masked[0], masked[1]], axis=0)
    left_imaginary = jnp.concatenate([masked[1], -masked[0]], axis=0)
    left_operand = jnp.concatenate([left_real, left_imaginary], axis=2)
    bins = receiver_traces.shape[2]
    width = receiver_traces.shape[3]
    right_side = receiver_traces.reshape(2 * receiver_traces.shape[1], bins, width)
    summed = lax.dot_general(
        left_operand, right_side, (((0,), (0,)), ((1,), (1,))), preferred_element_type=jnp.float32
    )
    cross_spectrum_product = (summed / valid_window_count).astype(jnp.bfloat16)
    return cross_spectrum_product.reshape(bins, 2, SRC, width)


def local(spectra, source_block, segment_flags):
    first_channel = source_block[0] * SRC
    owner_band = first_channel // RB
    offset = first_channel - owner_band * RB
    local_source = lax.dynamic_slice_in_dim(spectra, offset, SRC, 3)
    source = spread(local_source, "band", owner_band)
    valid_mask = segment_flags.astype(jnp.bfloat16)
    valid_window_count = jnp.sum(segment_flags).astype(jnp.float32)
    lag_weights = lag_table()
    cross_spectrum_product = stack_segment_windows(source, spectra, valid_mask, valid_window_count)
    lagged_correlation = lax.dot_general(
        lax.all_to_all(cross_spectrum_product, "chan", split_axis=3, concat_axis=0, tiled=True),
        lag_weights,
        (((0, 1), (0, 1)), ((), ())),
        preferred_element_type=jnp.float32,
    )
    return lagged_correlation[:, None]


def solution(mesh):
    return jax.shard_map(
        local,
        mesh=mesh,
        in_specs=(P(None, None, "chan", "band"), P(), P()),
        out_specs=P(None, "band", "chan", None),
        check_vma=False,
    )
```

profile of v0, /device:TPU:1, one launch (start us, length us, event | category | flops | bytes accessed | tf_op | source)
XLA Modules:
  0.0 246.4 jit_solution(11593618754978882445)
XLA Ops:
  6.5 0.0 copy-start
  6.5 0.0 all-reduce.2.cloned.1.call-start
  7.4 0.7 copy-done
  8.1 0.1 constant_dynamic-slice_fusion
  8.2 0.8 copy_select_fusion
  9.0 0.0 all-reduce.2.cloned.1.call-update
  9.0 1.4 fusion.20
  11.0 70.6 %all-reduce.2.cloned.1.call-done = bf16[2,30,16,64]{3,1,2,0:T(8,128)(2,1)} async-done(((bf16[2,30,16,64]{3,1,2,0:T(8,128)(2,1)}), bf16[2,30,16,64]{3,1,2,0:T(8,128)(2,1)}) %all-reduce.2.cloned.1.call-update) | async-done | bytes 122896 | tf_op jit(solution)/shard_map/psum | solution.py:16
  81.5 1.0 broadcast_multiply_fusion
  82.6 5.1 %divide_convert_fusion = bf16[16,128,1024]{2,1,0:T(8,128)(2,1)} fusion(f32[]{:T(128)S(6)} %convert_element_type.27, bf16[60,16,1024]{2,1,0:T(8,128)(2,1)S(1)} %bitcast.25, bf16[30,16,64]{2,0,1:T(8,128)(2,1)S(1)} %fusion.19, bf16[30,16,64]{2,0,1:T(8,128)(2,1)S(1)} %get-tuple-element.6, bf16[30,16,64]{2,0,1:T(8,128)(2,1)S(1)} %get-tuple-element.5), kind=kOutput, calls=%fused_computation | convolution fusion | flops 256835584 | bytes 6344708 | tf_op jit(solution)/shard_map/dot_general | solution.py:38
  87.7 20.3 %copy.16 = bf16[16,2,64,1024]{2,1,0,3:T(2,128)(2,1)} copy(bf16[16,2,64,1024]{3,2,1,0:T(8,128)(2,1)} %bitcast.30) | data formatting | bytes 8388608 | tf_op jit(solution)/shard_map/reshape | solution.py:42
  108.0 13.9 %reshape.165 = bf16[32,2,32768]{2,1,0:T(2,128)(2,1)} reshape(bf16[1024,16,2,64]{3,2,1,0:T(2,128)(2,1)} %bitcast.26) | data formatting | bytes 8388608
  121.9 12.1 %all-to-all-start = ((bf16[32,2,32768]{2,1,0:T(2,128)(2,1)}), bf16[32,2,32768]{2,1,0:T(2,128)(2,1)}, u32[]{:S(2)}, u32[]{:S(2)}) async-start(bf16[32,2,32768]{2,1,0:T(2,128)(2,1)} %reshape.165), calls=%async_computation | async-start | bytes 8388608 | tf_op jit(solution)/shard_map/all_to_all | solution.py:56
  134.1 9.4 %multiply_convert_fusion.1 = (bf16[512,1,1024]{2,0,1:T(8,128)(2,1)S(1)}, bf16[512,1,1024]{2,0,1:T(8,128)(2,1)}) fusion(s32[1024]{0:T(1024)S(1)} %iota_add_fusion, f32[512]{0:T(512)S(1)} %get-tuple-element.11, f32[512]{0:T(512)S(1)} %get-tuple-element.12), kind=kLoop, calls=%fused_computation.13 | loop fusion | flops 9437184 | bytes 2105344 | tf_op jit(solution)/shard_map/convert
  143.4 40.8 %all-to-all-done = bf16[32,2,32768]{2,1,0:T(2,128)(2,1)} async-done(((bf16[32,2,32768]{2,1,0:T(2,128)(2,1)}), bf16[32,2,32768]{2,1,0:T(2,128)(2,1)}, u32[]{:S(2)}, u32[]{:S(2)}) %all-to-all-start) | async-done | bytes 4194336 | tf_op jit(solution)/shard_map/all_to_all | solution.py:56
  184.2 13.6 %reshape.166 = bf16[1024,16,2,64]{3,2,1,0:T(2,128)(2,1)} reshape(bf16[32,2,32768]{2,1,0:T(2,128)(2,1)} %all-to-all-done) | data formatting | bytes 8388608
  197.8 9.8 %copy.17 = bf16[16,2,64,1024]{2,3,1,0:T(8,128)(2,1)} copy(bf16[16,2,64,1024]{2,1,0,3:T(2,128)(2,1)} %bitcast.27) | data formatting | bytes 8388608 | tf_op jit(solution)/shard_map/all_to_all | solution.py:56
  207.6 9.5 %copy.18 = bf16[32,16,2,64,32]{3,4,2,1,0:T(8,128)(2,1)} copy(bf16[32,16,2,64,32]{3,4,0,2,1:T(8,128)(2,1)} %bitcast.28) | data formatting | bytes 8388608 | tf_op jit(solution)/shard_map/all_to_all | solution.py:56
  217.1 12.0 %copy.19 = bf16[512,2,64,32]{0,3,1,2:T(8,128)(2,1)} copy(bf16[512,2,64,32]{2,3,1,0:T(8,128)(2,1)} %bitcast.29) | data formatting | bytes 8388608 | tf_op jit(solution)/shard_map/all_to_all | solution.py:56
  229.1 10.4 %convolution_bitcast_fusion = f32[64,1,32,1024]{3,2,1,0:T(8,128)} fusion(bf16[512,2,64,32]{0,3,1,2:T(8,128)(2,1)} %copy.19, bf16[512,1,1024]{2,0,1:T(8,128)(2,1)} %get-tuple-element.8, bf16[512,1,1024]{2,0,1:T(8,128)(2,1)S(1)} %get-tuple-element.7), kind=kOutput, calls=%fused_computation.1 | convolution fusion | flops 4296015872 | bytes 14680064 | tf_op jit(solution)/shard_map/dot_general | solution.py:55
  (4 shorter events, 0.0 us)
Async XLA Ops:
  6.5 1.6 copy-start
  6.5 75.0 %all-reduce.2.cloned.1.call-start = ((), (), s32[]{:S(2)}) async-start(), calls=%async_computation.1 | async-start | bytes 524288 | tf_op jit(solution)/shard_map/psum | solution.py:16
  121.9 62.3 %all-to-all-start = ((bf16[32,2,32768]{2,1,0:T(2,128)(2,1)}), bf16[32,2,32768]{2,1,0:T(2,128)(2,1)}, u32[]{:S(2)}, u32[]{:S(2)}) async-start(bf16[32,2,32768]{2,1,0:T(2,128)(2,1)} %reshape.165), calls=%async_computation | async-start | bytes 8388608 | tf_op jit(solution)/shard_map/all_to_all | solution.py:56
Sparse Core Ops, SparseCore 0:
  9.7 71.7 all-reduce.1
where the time goes:
time: 250 us; the launch traced here: 246 us
  waiting for transfers between devices  111 us (44%)
  local copies, waits for them, and re-layouts  80 us (32%)
  matrix products  15.5 us (6%)
  between operations  14.8 us (6%)
  other arithmetic  12.5 us (5%)
  starting transfers between devices  12.1 us (5%)
    psum x1, waiting for transfers between devices, spread(): return lax.psum(block, axis)  70.6 us
    all_to_all x1, waiting for transfers between devices, local(): lax.all_to_all(cross_spectrum_product, 'chan', split_axis=3, concat_axis=...  40.8 us
    all_to_all x3, local copies, waits for them, and re-layouts, local(): lax.all_to_all(cross_spectrum_product, 'chan', split_axis=3, concat_axis=...  31.3 us
    unnamed x4, local copies, waits for them, and re-layouts  28.3 us
    reshape x1, local copies, waits for them, and re-layouts, stack_segment_windows(): return cross_spectrum_product.reshape(bins, 2, SRC, width)  20.3 us
    all_to_all x1, starting transfers between devices, local(): lax.all_to_all(cross_spectrum_product, 'chan', split_axis=3, concat_axis=...  12.1 us
    dot_general x1, matrix products, local(): lax.dot_general(lax.all_to_all(cross_spectrum_product, 'chan', split_axis...  10.4 us
    another operation x1, other arithmetic  9.35 us
  transfers between devices with their start and end apart: 2, of which 2 were waited for; matrix products, arithmetic and copies ran while one was open for 4% of the time, Pallas kernels for 0%

commit v1 on v0

v1 whole, which is shorter than its diff:
```python
import functools
import math

import jax
import jax.numpy as jnp
from jax import lax
from jax.experimental import pallas as pl
from jax.experimental.pallas import tpu as pltpu
from jax.sharding import PartitionSpec as P

LAGS = 1024
SEG = 30
SRC = 64
BINS = 16
RX = 32
MESH = pl.DeviceIdType.MESH


def lag_table(bands, chans):
    per = BINS // bands
    bins = BINS * chans
    row = jnp.arange(bins, dtype=jnp.int32)
    frequency = row % chans * BINS + row // (per * chans) * per + row // chans % per
    frequency = frequency[:, None]
    lag = jnp.arange(LAGS, dtype=jnp.int32)[None, :] - LAGS // 2
    phase = 2.0 * math.pi / LAGS * (frequency * lag % LAGS).astype(jnp.float32)
    weight = jnp.where(frequency == 0, 1.0, 2.0).astype(jnp.float32) / jnp.sqrt(jnp.float32(LAGS))
    return jnp.concatenate([weight * jnp.cos(phase), -weight * jnp.sin(phase)], axis=0).astype(jnp.bfloat16)


def pack_kernel(tiles, chans, bands, band_ref, block_ref, flags_ref, x_ref, xs_ref, cand_ref, scale_ref, following):
    segs = 8 * tiles
    depth = BINS * segs
    rows = BINS // bands * segs
    f32, bf16 = jnp.float32, jnp.bfloat16

    following[SEG] = SEG

    def link(i, valid):
        g = SEG - 1 - i
        following[g] = jnp.where(flags_ref[g] > 0, g, following[g + 1])
        return valid + flags_ref[g]

    valid = lax.fori_loop(0, SEG, link, 0)

    def pack(k, at):
        g = jnp.minimum(at, SEG - 1)
        place = pl.ds(pl.multiple_of(k * BINS, BINS), BINS)
        xs_ref[0, place, :] = x_ref[0, g]
        xs_ref[1, place, :] = x_ref[1, g]
        return following[jnp.minimum(at + 1, SEG)]

    lax.fori_loop(0, segs, pack, following[0])

    r_i = lax.broadcasted_iota(jnp.int32, (depth, depth), 0)
    c_i = lax.broadcasted_iota(jnp.int32, (depth, depth), 1)
    to_bins = (r_i == (c_i & (BINS - 1)) * segs + (c_i >> 4)).astype(bf16)

    first = block_ref[0] * SRC
    width = RX * chans
    owner = first // width
    within = first - owner * width
    lane0 = pl.multiple_of(within // 128 * 128, 128)
    upper = (within // SRC) % 2
    sr = xs_ref[0, :, pl.ds(lane0, 128)].astype(f32)
    si = xs_ref[1, :, pl.ds(lane0, 128)].astype(f32)
    lane = lax.broadcasted_iota(jnp.int32, (depth, 128), 1)
    slot = lax.broadcasted_iota(jnp.int32, (depth, 128), 0) >> 4
    low = jnp.where(lane < SRC, sr, pltpu.roll(si, SRC, 1))
    high = jnp.where(lane < SRC, pltpu.roll(sr, SRC, 1), si)
    mine = jnp.where(upper == 0, low, high)
    count = jnp.where(owner == band_ref[0], valid, 0)
    mine = jnp.where(slot < count, mine, 0.0).astype(bf16)
    cand_ref[...] = jnp.dot(to_bins, mine, preferred_element_type=f32).astype(bf16).reshape(bands, rows, 128)
    scale_ref[...] = 1.0 / jnp.full((8, 128), valid, jnp.int32).astype(f32)


def stack_kernel(
    tiles, chans, bands,
    xs, cand, scale_ref, out_ref,
    send, recv, parts, zall, wide, cross,
    a2a_send, a2a_recv, rs_send, rs_recv, ag_send, ag_recv,
    right_send, right_recv, left_send, left_recv, sib_send, sib_recv,
):
    segs = 8 * tiles
    depth = BINS * segs
    per = BINS // bands
    rows = per * segs
    half = chans // 2
    c = lax.axis_index("chan")
    b = lax.axis_index("band")
    f32, bf16 = jnp.float32, jnp.bfloat16

    barrier = pltpu.get_barrier_semaphore()

    def greet_chan(i, carry):
        pl.semaphore_signal(barrier, inc=1, device_id=(lax.rem(c + i, chans), b), device_id_type=MESH)
        return carry

    def greet_band(i, carry):
        pl.semaphore_signal(barrier, inc=1, device_id=(c, lax.rem(b + i, bands)), device_id_type=MESH)
        return carry

    lax.fori_loop(1, chans, greet_chan, 0)
    lax.fori_loop(1, bands, greet_band, 0)

    c_i = lax.broadcasted_iota(jnp.int32, (depth, depth), 1)
    r_i = lax.broadcasted_iota(jnp.int32, (depth, depth), 0)
    from_segs = (c_i == (r_i & (BINS - 1)) * segs + (r_i >> 4)).astype(bf16)

    pl.semaphore_wait(barrier, chans + bands - 2)

    def rs_copy(other, slot_):
        return pltpu.make_async_remote_copy(
            src_ref=cand.at[other], dst_ref=parts.at[slot_],
            send_sem=rs_send.at[other], recv_sem=rs_recv.at[slot_],
            device_id=(c, other), device_id_type=MESH)

    def rs_start(i, carry):
        rs_copy(lax.rem(b + i, bands), b).start()
        return carry

    lax.fori_loop(1, bands, rs_start, 0)

    def a2a_copy(dest, origin):
        return pltpu.make_async_remote_copy(
            src_ref=send.at[dest], dst_ref=recv.at[origin],
            send_sem=a2a_send.at[dest], recv_sem=a2a_recv.at[origin],
            device_id=(dest, b), device_id_type=MESH)

    groups = chans // 4

    def turn(i, carry):
        block = lax.rem(c // 4 + i, groups)
        lanes = pl.ds(pl.multiple_of(block * 128, 128), 128)
        for comp in range(2):
            turned = jnp.dot(xs[comp, :, lanes].T, from_segs, preferred_element_type=f32).astype(bf16)
            for q in range(4):
                send[4 * block + q, comp * RX:(comp + 1) * RX, :] = turned[q * RX:(q + 1) * RX]
        for q in range(4):
            dest = 4 * block + q

            @pl.when(dest != c)
            def _():
                a2a_copy(dest, c).start()
        return carry

    lax.fori_loop(0, groups, turn, 0)
    recv[c] = send[c]

    def rs_sum(i, total):
        other = lax.rem(b + i, bands)
        rs_copy(other, other).wait_recv()
        return total + parts[other].astype(f32)

    zall[b, c] = lax.fori_loop(1, bands, rs_sum, cand[b].astype(f32)).astype(bf16)

    def ag_copy(dest, origin):
        return pltpu.make_async_remote_copy(
            src_ref=zall.at[b, origin], dst_ref=zall.at[b, origin],
            send_sem=ag_send.at[dest], recv_sem=ag_recv.at[origin],
            device_id=(dest, b), device_id_type=MESH)

    def ag_start(i, carry):
        ag_copy(lax.rem(c + i, chans), c).start()
        return carry

    lax.fori_loop(1, chans, ag_start, 0)

    def ag_wait(i, carry):
        other = lax.rem(c + i, chans)
        ag_copy(other, other).wait_recv()
        return carry

    lax.fori_loop(1, chans, ag_wait, 0)

    core = lax.rem(c, 2)
    twin = c + 1 - 2 * core
    right = lax.rem(b + 1, bands)
    left = lax.rem(b + bands - 1, bands)
    last = bands // 2

    def piece(origin, start, size):
        return zall.at[origin, pl.ds(start, size)]

    def hop(step, way, which):
        origin = lax.rem(b + bands - way * (step - 1 + which), bands)
        start, size = half * core, half
        if step == last:
            size = half // 2
            if way < 0:
                start = start + size
        ref = piece(origin, start, size)
        sems = (right_send, right_recv) if way > 0 else (left_send, left_recv)
        return pltpu.make_async_remote_copy(
            src_ref=ref, dst_ref=ref, send_sem=sems[0].at[step - 1], recv_sem=sems[1].at[step - 1],
            device_id=(c, right if way > 0 else left), device_id_type=MESH)

    def share(step, way, own):
        origin = lax.rem(b + bands - way * step, bands)
        start, size = half * (core if own else 1 - core), half
        if step == last:
            size = half // 2
            if way < 0:
                start = start + size
        ref = piece(origin, start, size)
        k = 2 * (step - 1) + (0 if way > 0 else 1)
        return pltpu.make_async_remote_copy(
            src_ref=ref, dst_ref=ref, send_sem=sib_send.at[k], recv_sem=sib_recv.at[k],
            device_id=(twin, b), device_id_type=MESH)

    wide[...] = jnp.zeros_like(wide)
    inverse = jnp.broadcast_to(scale_ref[0:1, :], (RX, 128))
    sign = jnp.where(lax.broadcasted_iota(jnp.int32, (RX, 128), 1) < SRC, inverse, -inverse)
    row_bin = lax.broadcasted_iota(jnp.int32, (rows, 128), 0)

    def stack(origin):
        place = pl.ds(pl.multiple_of(origin * rows, rows), rows)

        def chunk(j, carry):
            z = zall[origin, j]
            for p in range(per):
                inside = (row_bin >= p * segs) & (row_bin < (p + 1) * segs)
                wide[place, p * 128:(p + 1) * 128] = jnp.where(inside, z, jnp.zeros_like(z))
            product = jnp.dot(recv[j], wide[...], preferred_element_type=f32)
            for p in range(per):
                same = product[:RX, p * 128:(p + 1) * 128]
                swapped = pltpu.roll(product[RX:, p * 128:(p + 1) * 128], SRC, 1)
                cross[origin * (per * chans) + p * chans + j] = same * inverse + swapped * sign
            return carry

        lax.fori_loop(0, chans, chunk, 0)
        wide[place, :] = jnp.zeros((rows, per * 128), bf16)

    def a2a_wait(i, carry):
        other = lax.rem(c + i, chans)
        a2a_copy(other, other).wait_recv()
        return carry

    for step in range(1, last + 1):
        for way in (1, -1):
            hop(step, way, 0).start()
        for way in (1, -1):
            hop(step, way, 1).wait_recv()
            share(step, way, True).start()

    lax.fori_loop(1, chans, a2a_wait, 0)
    for step in range(1, last + 1):
        for way in (1, -1):
            share(step, way, False).wait_recv()

    def stack_all(i, carry):
        stack(i)
        return carry

    lax.fori_loop(0, bands, stack_all, 0)

    bins = BINS * chans

    def turn_back(r, carry):
        flat = cross[:, r, :].astype(bf16).T
        out_ref[r // 8, lax.rem(r, 8), :, :bins] = flat[:SRC]
        out_ref[r // 8, lax.rem(r, 8), :, bins:] = flat[SRC:]
        return carry

    lax.fori_loop(0, RX, turn_back, 0)

    def rs_done(i, carry):
        rs_copy(lax.rem(b + i, bands), b).wait_send()
        return carry

    def chan_done(i, carry):
        other = lax.rem(c + i, chans)
        a2a_copy(other, c).wait_send()
        ag_copy(other, c).wait_send()
        return carry

    lax.fori_loop(1, bands, rs_done, 0)
    lax.fori_loop(1, chans, chan_done, 0)
    for step in range(1, last + 1):
        for way in (1, -1):
            hop(step, way, 0).wait_send()
            share(step, way, True).wait_send()


def stacked(tiles, chans, bands, block, flags, x):
    segs = 8 * tiles
    depth = BINS * segs
    per = BINS // bands
    rows = per * segs
    bins = BINS * chans
    last = bands // 2
    dma = pltpu.SemaphoreType.DMA
    bf16 = jnp.bfloat16
    flops = 2 * chans * bands * 2 * RX * depth * per * 128
    vmem = pl.BlockSpec(memory_space=pltpu.VMEM)
    smem = pl.BlockSpec(memory_space=pltpu.SMEM)
    packed = pl.pallas_call(
        functools.partial(pack_kernel, tiles, chans, bands),
        out_shape=(
            jax.ShapeDtypeStruct((2, depth, RX * chans), bf16),
            jax.ShapeDtypeStruct((bands, rows, 128), bf16),
            jax.ShapeDtypeStruct((8, 128), jnp.float32),
        ),
        in_specs=[smem, smem, smem, vmem],
        out_specs=(vmem, vmem, vmem),
        scratch_shapes=[pltpu.SMEM((32,), jnp.int32)],
        compiler_params=pltpu.CompilerParams(vmem_limit_bytes=24 * 1024 * 1024),
    )(lax.axis_index("band").reshape(1), block, flags, x)
    return pl.pallas_call(
        functools.partial(stack_kernel, tiles, chans, bands),
        out_shape=jax.ShapeDtypeStruct((RX // 8, 8, SRC, 2 * bins), bf16),
        in_specs=[vmem] * 3,
        out_specs=vmem,
        scratch_shapes=[
            pltpu.VMEM((chans, 2 * RX, depth), bf16),
            pltpu.VMEM((chans, 2 * RX, depth), bf16),
            pltpu.VMEM((bands, rows, 128), bf16),
            pltpu.VMEM((bands, chans, rows, 128), bf16),
            pltpu.VMEM((depth, per * 128), bf16),
            pltpu.VMEM((bins, RX, 128), jnp.float32),
            dma((chans,)), dma((chans,)), dma((bands,)), dma((bands,)), dma((chans,)), dma((chans,)),
            dma((last,)), dma((last,)), dma((last,)), dma((last,)), dma((2 * last,)), dma((2 * last,)),
        ],
        compiler_params=pltpu.CompilerParams(
            collective_id=tiles, has_side_effects=True, vmem_limit_bytes=48 * 1024 * 1024
        ),
        cost_estimate=pl.CostEstimate(flops=flops, bytes_accessed=8 * 1024 * 1024, transcendentals=0),
    )(*packed)


def lag_kernel(cross_ref, weights_ref, out_ref):
    k = weights_ref.shape[0]
    left = cross_ref[0].reshape(8 * SRC, k)
    result = jnp.dot(left, weights_ref[...], preferred_element_type=jnp.float32)
    result = result.reshape(8, SRC, LAGS)
    for r in range(8):
        out_ref[:, 0, r, :] = result[r]


def correlate(cross, weights):
    k = weights.shape[0]
    return pl.pallas_call(
        lag_kernel,
        grid=(RX // 8,),
        out_shape=jax.ShapeDtypeStruct((SRC, 1, RX, LAGS), jnp.float32),
        in_specs=[
            pl.BlockSpec((1, 8, SRC, k), lambda i: (i, 0, 0, 0)),
            pl.BlockSpec((k, LAGS), lambda i: (0, 0)),
        ],
        out_specs=pl.BlockSpec((SRC, 1, 8, LAGS), lambda i: (0, 0, i, 0)),
        compiler_params=pltpu.CompilerParams(vmem_limit_bytes=32 * 1024 * 1024),
        cost_estimate=pl.CostEstimate(
            flops=2 * SRC * RX * k * LAGS, bytes_accessed=16 * 1024 * 1024, transcendentals=0
        ),
    )(cross, weights)


def solution(mesh):
    chans, bands = mesh.shape["chan"], mesh.shape["band"]

    def local(spectra, source_block, segment_flags):
        valid = jnp.sum(segment_flags)
        tier = (valid > 16).astype(jnp.int32) + (valid > 24).astype(jnp.int32)
        cross = lax.switch(
            tier,
            [functools.partial(stacked, tiles, chans, bands) for tiles in (2, 3, 4)],
            source_block, segment_flags, spectra,
        )
        return correlate(cross, lag_table(bands, chans))

    return jax.shard_map(
        local,
        mesh=mesh,
        in_specs=(P(None, None, "chan", "band"), P(), P()),
        out_specs=P(None, "band", "chan", None),
        check_vma=False,
    )
```

time: 250 us -> 149 us (0.60); the launches traced: 246 us -> 149 us
  Pallas kernels: 0 us -> 137 us
  waiting for transfers between devices: 111 us -> 0 us
  local copies, waits for them, and re-layouts: 80 us -> 0.01 us
  matrix products: 15.5 us -> 0 us
  between operations: 14.8 us -> 1.35 us
  starting transfers between devices: 12.1 us -> 0 us
    pallas_call x0 -> x3, Pallas kernels: none -> 137 us  [the longest x1 124 us: stacked(): pl.pallas_call(functools.partial(stack_kernel, tiles, chans, bands), out_...]
    psum x1 -> x0, waiting for transfers between devices: 70.6 us -> none  [spread(): return lax.psum(block, axis)]
    all_to_all x1 -> x0, waiting for transfers between devices: 40.8 us -> none  [local(): lax.all_to_all(cross_spectrum_product, 'chan', split_axis=3, concat_axis=...]
    all_to_all x3 -> x0, local copies, waits for them, and re-layouts: 31.3 us -> none  [local(): lax.all_to_all(cross_spectrum_product, 'chan', split_axis=3, concat_axis=...]
    unnamed x4 -> x2, local copies, waits for them, and re-layouts: 28.3 us -> 0.01 us
    reshape x1 -> x0, local copies, waits for them, and re-layouts: 20.3 us -> none  [stack_segment_windows(): return cross_spectrum_product.reshape(bins, 2, SRC, width)]
    dot_general x2 -> x0, matrix products: 15.5 us -> none  [the longest x1 10.4 us: local(): lax.dot_general(lax.all_to_all(cross_spectrum_product, 'chan', split_axis...]
    all_to_all x1 -> x0, starting transfers between devices: 12.1 us -> none  [local(): lax.all_to_all(cross_spectrum_product, 'chan', split_axis=3, concat_axis=...]
  transfers between devices with their start and end apart: 2 -> 0, of which waited for: 2 -> 0; matrix products, arithmetic and copies ran while one was open for 4% -> 0% of each run, Pallas kernels for 0% -> 0%
where the time goes in v1:
time: 149 us
  Pallas kernels  137 us (92%)
  other arithmetic  10.7 us (7%)
    pallas_call x1, Pallas kernels, stacked(): pl.pallas_call(functools.partial(stack_kernel, tiles, chans, bands), out_...  124 us
    pallas_call x1, Pallas kernels, correlate(): pl.pallas_call(lag_kernel, grid=(RX // 8,), out_shape=jax.ShapeDtypeStruc...  10 us
    another operation x1, other arithmetic  9.19 us

profile of v1, /device:TPU:1, one launch (start us, length us, event | category | flops | bytes accessed | tf_op | source)
XLA Modules:
  0.0 149.0 jit_solution(88550673086225109)
XLA Ops:
  0.0 0.0 copy-start
  0.0 1.4 reduce_sum.9
  2.7 9.2 %multiply_convert_fusion.1 = (bf16[512,1024]{1,0:T(8,128)(2,1)S(1)}, bf16[512,1024]{1,0:T(8,128)(2,1)S(1)}) fusion(s32[1024]{0:T(1024)S(1)} %iota_add_fusion, s32[512]{0:T(512)S(1)} %fusion.9, f32[512]{0:T(512)S(1)} %get-tuple-element.47, f32[512]{0:T(512)S(1)} %get-tuple-element.48), kind=kLoop, calls=%fused_computation.10 | loop fusion | flops 9437184 | bytes 2107392 | tf_op jit(solution)/shard_map/convert
  11.9 0.0 copy-done
  11.9 0.2 pad_maximum_fusion.weights_ref
  12.1 126.9 %conditional.1 = (bf16[4,8,64,1024]{3,2,1,0:T(8,128)(2,1)}) conditional(s32[]{:T(128)} %clamp.3, (s32[1]{0:T(128)}, s32[30]{0:T(128)S(1)}, bf16[2,30,16,1024]{3,2,1,0:T(8,128)(2,1)}) %tuple.20, (s32[1]{0:T(128)}, s32[30]{0:T(128)S(1)}, bf16[2,30,16,1024]{3,2,1,0:T(8,128)(2,1)}) %tuple.21, (s32[1]{0:T(128)}, s32[30]{0:T(128)S(1)}, ...), branch_computations={%region_1.0_spmd, %region_2.0_spmd, %region_3.0_spmd} | conditional | flops 4294967296 | bytes 8388636 | solution.py:365
  12.1 2.8 %branch_0_fun.2 = (bf16[2,256,1024]{2,1,0:T(8,128)(2,1)S(1)}, bf16[8,32,128]{2,1,0:T(8,128)(2,1)S(1)}, f32[8,128]{1,0:T(8,128)S(1)}) custom-call(s32[1]{0:T(128)} %bitcast.band_ref, s32[1]{0:T(128)} %get-tuple-element.26.block_ref, s32[30]{0:T(128)S(1)} %get-tuple-element.28.flags_ref, bf16[2,30,16,1024]{3,2,1,0:T(8,128)(2,1)} %get-tuple-element.29.x_ref), custom_call_target="tpu_custom_call" | custom-call | tf_op jit(solution)/shard_map/cond/branch_0_fun/pallas_call | solution.py:298
  15.0 124.0 %branch_0_fun.3 = bf16[4,8,64,1024]{3,2,1,0:T(8,128)(2,1)} custom-call(bf16[2,256,1024]{2,1,0:T(8,128)(2,1)S(1)} %get-tuple-element.30.xs, bf16[8,32,128]{2,1,0:T(8,128)(2,1)S(1)} %get-tuple-element.31.cand, f32[8,128]{1,0:T(8,128)S(1)} %get-tuple-element.32.scale_ref), custom_call_target="tpu_custom_call" | custom-call | flops 2147483648 | bytes 8388608 | tf_op jit(solution)/shard_map/cond/branch_0_fun/pallas_call | solution.py:310
  139.0 10.0 %shard_map.37 = f32[64,1,32,1024]{3,2,1,0:T(8,128)} custom-call(bf16[4,8,64,1024]{3,2,1,0:T(8,128)(2,1)} %get-tuple-element.49.cross_ref, bf16[1024,1024]{1,0:T(8,128)(2,1)S(1)} %pad_maximum_fusion.weights_ref), custom_call_target="tpu_custom_call" | custom-call | flops 4294967296 | bytes 16777216 | tf_op jit(solution)/shard_map/pallas_call | solution.py:343
  (3 shorter events, 0.0 us)
Async XLA Ops:
  0.0 11.9 %copy-start = (s32[30]{0:T(128)S(1)}, s32[30]{0:T(128)}, u32[]{:S(2)}) copy-start(s32[30]{0:T(128)} %param.8) | copy-start | bytes 364

commit v2 on v1

v2 whole, which is shorter than its diff:
```python
import functools
import math

import jax
import jax.numpy as jnp
from jax import lax
from jax.experimental import pallas as pl
from jax.experimental.pallas import tpu as pltpu
from jax.sharding import PartitionSpec as P

LAGS = 1024
SEG = 30
SRC = 64
BINS = 16
RX = 32
MESH = pl.DeviceIdType.MESH


def lag_rows(parity, start, count):
    shape = (count, LAGS // 2)
    frequency = 2 * (start + lax.broadcasted_iota(jnp.int32, shape, 0)) + parity
    lag = lax.broadcasted_iota(jnp.int32, shape, 1)
    phase = (frequency * (lag + LAGS // 2)) & (LAGS - 1)
    quarter = (phase + LAGS // 8) >> 8
    angle = (phase - (quarter << 8)).astype(jnp.float32) * (2.0 * math.pi / LAGS)
    square = angle * angle
    sine = angle * (1 + square * (-1 / 6 + square * (1 / 120 + square * (-1 / 5040 + square * (1 / 362880)))))
    cosine = 1 + square * (-1 / 2 + square * (1 / 24 + square * (-1 / 720 + square * (1 / 40320))))
    swap = (quarter & 1) == 1
    cos_part = jnp.where(swap, sine, cosine)
    sin_part = jnp.where(swap, cosine, sine)
    weight = jnp.where(frequency == 0, 1.0, 2.0) * (1.0 / math.sqrt(LAGS))
    cos_part = jnp.where(((quarter + 1) & 2) == 2, -cos_part, cos_part) * weight
    sin_part = jnp.where((quarter & 2) == 2, sin_part, -sin_part) * weight
    return cos_part.astype(jnp.bfloat16), sin_part.astype(jnp.bfloat16)


def pack_kernel(tiles, chans, bands, band_ref, block_ref, flags_ref, x_ref, xs_ref, cand_ref, scale_ref, following):
    segs = 8 * tiles
    depth = BINS * segs
    rows = depth // bands
    f32, bf16 = jnp.float32, jnp.bfloat16

    following[SEG] = SEG

    def link(i, valid):
        g = SEG - 1 - i
        following[g] = jnp.where(flags_ref[g] > 0, g, following[g + 1])
        return valid + flags_ref[g]

    valid = lax.fori_loop(0, SEG, link, 0)

    def pack(k, at):
        g = jnp.minimum(at, SEG - 1)
        place = pl.ds(pl.multiple_of(k * BINS, BINS), BINS)
        xs_ref[0, place, :] = x_ref[0, g]
        xs_ref[1, place, :] = x_ref[1, g]
        return following[jnp.minimum(at + 1, SEG)]

    lax.fori_loop(0, segs, pack, following[0])

    first = block_ref[0] * SRC
    width = RX * chans
    owner = first // width
    within = first - owner * width
    lane0 = pl.multiple_of(within // 128 * 128, 128)
    upper = (within // SRC) % 2
    sr = xs_ref[0, :, pl.ds(lane0, 128)].astype(f32)
    si = xs_ref[1, :, pl.ds(lane0, 128)].astype(f32)
    lane = lax.broadcasted_iota(jnp.int32, (depth, 128), 1)
    slot = lax.broadcasted_iota(jnp.int32, (depth, 128), 0) >> 4
    low = jnp.where(lane < SRC, sr, pltpu.roll(si, SRC, 1))
    high = jnp.where(lane < SRC, pltpu.roll(sr, SRC, 1), si)
    mine = jnp.where(upper == 0, low, high)
    count = jnp.where(owner == band_ref[0], valid, 0)
    mine = jnp.where(slot < count, mine, 0.0).astype(bf16)
    cand_ref[...] = mine.reshape(bands, rows, 128)
    scale_ref[...] = 1.0 / jnp.full((8, 128), valid, jnp.int32).astype(f32)


def stack_kernel(
    tiles, chans, bands,
    xs, cand, scale_ref, cross_out, table_out,
    send, recv, parts, zall, spread, cross, turned, table,
    a2a_send, a2a_recv, rs_send, rs_recv, ag_send, ag_recv,
    right_send, right_recv, left_send, left_recv, sib_send, sib_recv, out_sem,
):
    depth = BINS * 8 * tiles
    bins = BINS * chans
    half = chans // 2
    pieces = max(1, half // 4)
    size = half // pieces
    last = bands // 2
    groups = chans // 4
    c = lax.axis_index("chan")
    b = lax.axis_index("band")
    f32, bf16 = jnp.float32, jnp.bfloat16

    barrier = pltpu.get_barrier_semaphore()

    def greet_chan(i, carry):
        pl.semaphore_signal(barrier, inc=1, device_id=(lax.rem(c + i, chans), b), device_id_type=MESH)
        return carry

    def greet_band(i, carry):
        pl.semaphore_signal(barrier, inc=1, device_id=(c, lax.rem(b + i, bands)), device_id_type=MESH)
        return carry

    lax.fori_loop(1, bands, greet_band, 0)
    lax.fori_loop(1, chans, greet_chan, 0)

    def turn(block, carry):
        lanes = pl.ds(pl.multiple_of(block * 128, 128), 128)
        for comp in range(2):
            rows = xs[comp, :, lanes].T
            for q in range(4):
                send[4 * block + q, comp * RX:(comp + 1) * RX, :] = rows[q * RX:(q + 1) * RX]
        return carry

    lax.fori_loop(0, groups, turn, 0)
    recv[c] = send[c]

    pl.semaphore_wait(barrier, chans + bands - 2)

    def rs_copy(other, slot):
        return pltpu.make_async_remote_copy(
            src_ref=cand.at[other], dst_ref=parts.at[slot],
            send_sem=rs_send.at[other], recv_sem=rs_recv.at[slot],
            device_id=(c, other), device_id_type=MESH)

    def rs_start(i, carry):
        rs_copy(lax.rem(b + i, bands), b).start()
        return carry

    lax.fori_loop(1, bands, rs_start, 0)

    count = min(32, bins // 2)

    def fill(i, carry):
        start = pl.multiple_of(i * count, count)
        for parity in range(2):
            cos_part, sin_part = lag_rows(parity, start, count)
            table[parity, pl.ds(start, count), :] = cos_part
            table[parity, pl.ds(bins // 2 + start, count), :] = sin_part
        return carry

    lax.fori_loop(0, bins // 2 // count, fill, 0)
    table_copy = pltpu.make_async_copy(table, table_out, out_sem.at[RX // 8])
    table_copy.start()

    def rs_sum(i, total):
        other = lax.rem(b + i, bands)
        rs_copy(other, other).wait_recv()
        return total + parts[other].astype(f32)

    zall[b, c] = lax.fori_loop(1, bands, rs_sum, cand[b].astype(f32)).astype(bf16)

    def ag_copy(dest, origin):
        return pltpu.make_async_remote_copy(
            src_ref=zall.at[b, origin], dst_ref=zall.at[b, origin],
            send_sem=ag_send.at[dest], recv_sem=ag_recv.at[origin],
            device_id=(dest, b), device_id_type=MESH)

    def ag_start(i, carry):
        ag_copy(lax.rem(c + i, chans), c).start()
        return carry

    lax.fori_loop(1, chans, ag_start, 0)

    def a2a_copy(dest, origin):
        return pltpu.make_async_remote_copy(
            src_ref=send.at[dest], dst_ref=recv.at[origin],
            send_sem=a2a_send.at[dest], recv_sem=a2a_recv.at[origin],
            device_id=(dest, b), device_id_type=MESH)

    def a2a_start(i, carry):
        a2a_copy(lax.rem(c + i, chans), c).start()
        return carry

    lax.fori_loop(1, chans, a2a_start, 0)

    def ag_wait(start, number):
        def one(i, carry):
            @pl.when(start + i != c)
            def _():
                ag_copy(start + i, start + i).wait_recv()
            return carry

        lax.fori_loop(0, number, one, 0)

    core = lax.rem(c, 2)
    twin = c + 1 - 2 * core
    right = lax.rem(b + 1, bands)
    left = lax.rem(b + bands - 1, bands)

    def part(origin, owner, piece, step, way):
        start, number = half * owner + size * piece, size
        if step == last:
            number = size // 2
            if way < 0:
                start = start + number
        return zall.at[origin, pl.ds(start, number)]

    def hop(piece, step, way, which):
        origin = lax.rem(b + bands - way * (step - 1 + which), bands)
        ref = part(origin, core, piece, step, way)
        sems = (right_send, right_recv) if way > 0 else (left_send, left_recv)
        return pltpu.make_async_remote_copy(
            src_ref=ref, dst_ref=ref, send_sem=sems[0].at[piece, step - 1], recv_sem=sems[1].at[piece, step - 1],
            device_id=(c, right if way > 0 else left), device_id_type=MESH)

    def share(piece, step, way, own):
        origin = lax.rem(b + bands - way * step, bands)
        ref = part(origin, core if own else 1 - core, piece, step, way)
        k = 2 * (step - 1) + (0 if way > 0 else 1)
        return pltpu.make_async_remote_copy(
            src_ref=ref, dst_ref=ref, send_sem=sib_send.at[piece, k], recv_sem=sib_recv.at[piece, k],
            device_id=(twin, b), device_id_type=MESH)

    def advance(piece, step):
        if step == 1:
            ag_wait(half * core + size * piece, size)
        else:
            for way in (1, -1):
                hop(piece, step - 1, way, 1).wait_recv()
        if step <= last:
            for way in (1, -1):
                hop(piece, step, way, 0).start()
        if step > 1:
            for way in (1, -1):
                share(piece, step - 1, way, True).start()

    def arrived(piece):
        ag_wait(half * (1 - core) + size * piece, size)
        for step in range(1, last + 1):
            for way in (1, -1):
                share(piece, step, way, False).wait_recv()

    inverse = jnp.broadcast_to(scale_ref[0:1, :], (8 * BINS, 128))
    row = lax.broadcasted_iota(jnp.int32, (BINS, depth), 0)
    row_bin = jnp.where(row < BINS // 2, 2 * row, 2 * row - (BINS - 1))
    kept = row_bin == (lax.broadcasted_iota(jnp.int32, (BINS, depth), 1) & (BINS - 1))
    sign = jnp.where(lax.broadcasted_iota(jnp.int32, (1, 128), 1) < SRC, 1.0, -1.0)

    def stack(j, buffer):
        @pl.when(j != c)
        def _():
            a2a_copy(j, j).wait_recv()
        z = zall[:, j].reshape(depth, 128)
        swapped = (pltpu.roll(z.astype(f32), SRC, 1) * sign).astype(bf16)
        weights = jnp.concatenate([z, swapped], axis=0)
        spread[buffer] = recv[j].astype(f32)
        place = pl.ds(pl.multiple_of(BINS // 2 * j, BINS // 2), BINS // 2)
        for g in range(RX // 8):
            left = []
            for r in range(8 * g, 8 * g + 8):
                line = []
                for comp in range(2):
                    value = jnp.broadcast_to(spread[buffer, comp * RX + r:comp * RX + r + 1, :], (BINS, depth))
                    line.append(jnp.where(kept, value, 0.0).astype(bf16))
                left.append(jnp.concatenate(line, axis=1))
            product = jnp.dot(jnp.concatenate(left, axis=0), weights, preferred_element_type=f32) * inverse
            product = product.reshape(8, BINS, 128)
            cross[0, 8 * g:8 * g + 8, place, :] = product[:, :BINS // 2]
            cross[1, 8 * g:8 * g + 8, place, :] = product[:, BINS // 2:]

    def stack_piece(owner, piece):
        def pair(i, carry):
            for k in range(2):
                stack(half * owner + size * piece + 2 * i + k, k)
            return carry

        lax.fori_loop(0, size // 2, pair, 0)

    first = list(range((pieces + 1) // 2))
    second = list(range((pieces + 1) // 2, pieces))
    for step in range(1, last + 1):
        for piece in first:
            advance(piece, step)
    for piece in second:
        advance(piece, 1)
    for piece in first:
        advance(piece, last + 1)
    for piece in first:
        arrived(piece)
    work = [(owner, piece) for piece in first for owner in range(2)]
    for step in range(2, last + 2):
        if work and second:
            stack_piece(*work.pop(0))
        for piece in second:
            advance(piece, step)
    for piece in second:
        arrived(piece)
    for owner, piece in work + [(owner, piece) for piece in second for owner in range(2)]:
        stack_piece(owner, piece)

    def out_copy(g):
        return pltpu.make_async_copy(turned.at[g], cross_out.at[g], out_sem.at[g])

    k = bins // 2
    for g in range(RX // 8):
        def turn_back(i, carry, g=g):
            for r in (2 * i, 2 * i + 1):
                for parity in range(2):
                    flat = cross[parity, 8 * g + r].astype(bf16).T
                    turned[g, r, :, 2 * parity * k:(2 * parity + 1) * k] = flat[:SRC]
                    turned[g, r, :, (2 * parity + 1) * k:(2 * parity + 2) * k] = flat[SRC:]
            return carry

        lax.fori_loop(0, 4, turn_back, 0)
        out_copy(g).start()

    def rs_done(i, carry):
        rs_copy(lax.rem(b + i, bands), b).wait_send()
        return carry

    def chan_done(i, carry):
        other = lax.rem(c + i, chans)
        a2a_copy(other, c).wait_send()
        ag_copy(other, c).wait_send()
        return carry

    lax.fori_loop(1, bands, rs_done, 0)
    lax.fori_loop(1, chans, chan_done, 0)
    for piece in range(pieces):
        for step in range(1, last + 1):
            for way in (1, -1):
                hop(piece, step, way, 0).wait_send()
                share(piece, step, way, True).wait_send()
    table_copy.wait()
    for g in range(RX // 8):
        out_copy(g).wait()


def stacked(tiles, chans, bands, block, flags, x):
    depth = BINS * 8 * tiles
    rows = depth // bands
    bins = BINS * chans
    pieces = max(1, chans // 8)
    last = bands // 2
    dma = pltpu.SemaphoreType.DMA
    f32, bf16 = jnp.float32, jnp.bfloat16
    vmem = pl.BlockSpec(memory_space=pltpu.VMEM)
    smem = pl.BlockSpec(memory_space=pltpu.SMEM)
    hbm = pl.BlockSpec(memory_space=pl.ANY)
    packed = pl.pallas_call(
        functools.partial(pack_kernel, tiles, chans, bands),
        out_shape=(
            jax.ShapeDtypeStruct((2, depth, RX * chans), bf16),
            jax.ShapeDtypeStruct((bands, rows, 128), bf16),
            jax.ShapeDtypeStruct((8, 128), f32),
        ),
        in_specs=[smem, smem, smem, vmem],
        out_specs=(vmem, vmem, vmem),
        scratch_shapes=[pltpu.SMEM((32,), jnp.int32)],
        compiler_params=pltpu.CompilerParams(vmem_limit_bytes=24 * 1024 * 1024),
    )(lax.axis_index("band").reshape(1), block, flags, x)
    flops = 2 * chans * RX * BINS * 2 * depth * 128
    return pl.pallas_call(
        functools.partial(stack_kernel, tiles, chans, bands),
        out_shape=(
            jax.ShapeDtypeStruct((RX // 8, 8, SRC, 2 * bins), bf16),
            jax.ShapeDtypeStruct((2, bins, LAGS // 2), bf16),
        ),
        in_specs=[vmem] * 3,
        out_specs=(hbm, hbm),
        scratch_shapes=[
            pltpu.VMEM((chans, 2 * RX, depth), bf16),
            pltpu.VMEM((chans, 2 * RX, depth), bf16),
            pltpu.VMEM((bands, rows, 128), bf16),
            pltpu.VMEM((bands, chans, rows, 128), bf16),
            pltpu.VMEM((2, 2 * RX, depth), f32),
            pltpu.VMEM((2, RX, bins // 2, 128), f32),
            pltpu.VMEM((RX // 8, 8, SRC, 2 * bins), bf16),
            pltpu.VMEM((2, bins, LAGS // 2), bf16),
            dma((chans,)), dma((chans,)), dma((bands,)), dma((bands,)), dma((chans,)), dma((chans,)),
            dma((pieces, last)), dma((pieces, last)), dma((pieces, last)), dma((pieces, last)),
            dma((pieces, 2 * last)), dma((pieces, 2 * last)), dma((RX // 8 + 1,)),
        ],
        compiler_params=pltpu.CompilerParams(
            collective_id=tiles, has_side_effects=True, vmem_limit_bytes=48 * 1024 * 1024
        ),
        cost_estimate=pl.CostEstimate(flops=flops, bytes_accessed=8 * 1024 * 1024, transcendentals=0),
    )(*packed)


def lag_kernel(cross_ref, weights_ref, out_ref):
    k = weights_ref.shape[1]
    left = cross_ref[0].reshape(8 * SRC, 2 * k)
    even = jnp.dot(left[:, :k], weights_ref[0], preferred_element_type=jnp.float32)
    odd = jnp.dot(left[:, k:], weights_ref[1], preferred_element_type=jnp.float32)
    low = (even + odd).reshape(8, SRC, LAGS // 2)
    high = (even - odd).reshape(8, SRC, LAGS // 2)
    for r in range(8):
        out_ref[:, 0, r, :LAGS // 2] = low[r]
        out_ref[:, 0, r, LAGS // 2:] = high[r]


def correlate(cross, weights):
    k = weights.shape[1]
    return pl.pallas_call(
        lag_kernel,
        grid=(RX // 8,),
        out_shape=jax.ShapeDtypeStruct((SRC, 1, RX, LAGS), jnp.float32),
        in_specs=[
            pl.BlockSpec((1, 8, SRC, 2 * k), lambda i: (i, 0, 0, 0)),
            pl.BlockSpec((2, k, LAGS // 2), lambda i: (0, 0, 0)),
        ],
        out_specs=pl.BlockSpec((SRC, 1, 8, LAGS), lambda i: (0, 0, i, 0)),
        compiler_params=pltpu.CompilerParams(vmem_limit_bytes=32 * 1024 * 1024),
        cost_estimate=pl.CostEstimate(
            flops=2 * SRC * RX * k * LAGS, bytes_accessed=16 * 1024 * 1024, transcendentals=0
        ),
    )(cross, weights)


def solution(mesh):
    chans, bands = mesh.shape["chan"], mesh.shape["band"]

    def local(spectra, source_block, segment_flags):
        valid = jnp.sum(segment_flags)
        tier = (valid > 16).astype(jnp.int32) + (valid > 24).astype(jnp.int32)
        cross, weights = lax.switch(
            tier,
            [functools.partial(stacked, tiles, chans, bands) for tiles in (2, 3, 4)],
            source_block, segment_flags, spectra,
        )
        return correlate(cross, weights)

    return jax.shard_map(
        local,
        mesh=mesh,
        in_specs=(P(None, None, "chan", "band"), P(), P()),
        out_specs=P(None, "band", "chan", None),
        check_vma=False,
    )
```

time: 149 us -> 80.9 us (0.54)
  Pallas kernels: 137 us -> 76.8 us
  other arithmetic: 10.7 us -> 1.29 us
    pallas_call x1, Pallas kernels: 124 us -> 65.7 us  [stacked(): pl.pallas_call(functools.partial(stack_kernel, tiles, chans, bands), out_...]
    another operation x1 -> x0, other arithmetic: 9.19 us -> none
    pallas_call x1, Pallas kernels: 10 us -> 8.42 us  [correlate(): pl.pallas_call(lag_kernel, grid=(RX // 8,), out_shape=jax.ShapeDtypeStruc...]
where the time goes in v2:
time: 80.9 us; the launch traced here: 79.7 us
  Pallas kernels  76.8 us (95%)
  between operations  1.31 us (2%)
  other arithmetic  1.29 us (2%)
    pallas_call x1, Pallas kernels, stacked(): pl.pallas_call(functools.partial(stack_kernel, tiles, chans, bands), out_...  65.7 us
    pallas_call x1, Pallas kernels, correlate(): pl.pallas_call(lag_kernel, grid=(RX // 8,), out_shape=jax.ShapeDtypeStruc...  8.42 us
    pallas_call x1, Pallas kernels, stacked(): pl.pallas_call(functools.partial(pack_kernel, tiles, chans, bands), out_s...  2.7 us

profile of v2, /device:TPU:1, one launch (start us, length us, event | category | flops | bytes accessed | tf_op | source)
XLA Modules:
  0.0 79.7 jit_solution(14972806735417904149)
XLA Ops:
  0.0 1.3 %reduce_sum.9 = s32[]{:T(128)} reduce(s32[30]{0:T(128)} %param.8, s32[]{:T(128)} %constant.4.clone.1), dimensions={0}, to_apply=%region_0.0 | reduce | flops 29 | bytes 128 | tf_op jit(solution)/shard_map/reduce_sum | solution.py:421
  2.6 68.6 %conditional.1 = ((bf16[4,8,64,1024]{3,2,1,0:T(8,128)(2,1)}, bf16[2,512,512]{2,1,0:T(8,128)(2,1)S(1)})) conditional(s32[]{:T(128)} %clamp.3, (s32[1]{0:T(128)}, s32[30]{0:T(128)}, bf16[2,30,16,1024]{3,2,1,0:T(8,128)(2,1)}) %tuple.14, (s32[1]{0:T(128)}, s32[30]{0:T(128)}, bf16[2,30,16,1024]{3,2,1,0:T(8,128)(2,1)}) %tuple.14, ...), branch_computations={%region_1.0_spmd, %region_2.0_spmd, %region_3.0_spmd} | conditional | flops 4294967296 | bytes 8388636 | solution.py:423
  2.6 2.7 %branch_0_fun.2 = (bf16[2,256,1024]{2,1,0:T(8,128)(2,1)S(1)}, bf16[8,32,128]{2,1,0:T(8,128)(2,1)S(1)}, f32[8,128]{1,0:T(8,128)S(1)}) custom-call(s32[1]{0:T(128)} %bitcast.band_ref, s32[1]{0:T(128)} %get-tuple-element.23.block_ref, s32[30]{0:T(128)} %get-tuple-element.24.flags_ref, bf16[2,30,16,1024]{3,2,1,0:T(8,128)(2,1)} %get-tuple-element.25.x_ref), custom_call_target="tpu_custom_call" | custom-call | tf_op jit(solution)/shard_map/cond/branch_0_fun/pallas_call | solution.py:346
  5.3 65.7 %branch_0_fun.3 = (bf16[4,8,64,1024]{3,2,1,0:T(8,128)(2,1)}, bf16[2,512,512]{2,1,0:T(8,128)(2,1)S(1)}) custom-call(bf16[2,256,1024]{2,1,0:T(8,128)(2,1)S(1)} %get-tuple-element.26.xs, bf16[8,32,128]{2,1,0:T(8,128)(2,1)S(1)} %get-tuple-element.27.cand, f32[8,128]{1,0:T(8,128)S(1)} %get-tuple-element.28.scale_ref), custom_call_target="tpu_custom_call" | custom-call | flops 2147483648 | bytes 8388608 | tf_op jit(solution)/shard_map/cond/branch_0_fun/pallas_call | solution.py:359
  71.2 8.4 %shard_map.37 = f32[64,1,32,1024]{3,2,1,0:T(8,128)} custom-call(bf16[4,8,64,1024]{3,2,1,0:T(8,128)(2,1)} %get-tuple-element.43.cross_ref, bf16[2,512,512]{2,1,0:T(8,128)(2,1)S(1)} %get-tuple-element.44.weights_ref), custom_call_target="tpu_custom_call" | custom-call | flops 2147483648 | bytes 16777216 | tf_op jit(solution)/shard_map/pallas_call | solution.py:401

commit v3 on v2

--- a/solution.py
+++ b/solution.py
@@ -81,7 +81,7 @@
 def stack_kernel(
     tiles, chans, bands,
     xs, cand, scale_ref, cross_out, table_out,
-    send, recv, parts, zall, spread, cross, turned, table,
+    send, recv, parts, own, zall, spread, cross, turned, table,
     a2a_send, a2a_recv, rs_send, rs_recv, ag_send, ag_recv,
     right_send, right_recv, left_send, left_recv, sib_send, sib_recv, out_sem,
 ):
@@ -153,19 +153,33 @@
         rs_copy(other, other).wait_recv()
         return total + parts[other].astype(f32)
 
-    zall[b, c] = lax.fori_loop(1, bands, rs_sum, cand[b].astype(f32)).astype(bf16)
+    core = lax.rem(c, 2)
+    twin = c + 1 - 2 * core
+    holder = c // half
+    own[...] = lax.fori_loop(1, bands, rs_sum, cand[b].astype(f32)).astype(bf16)
+
+    @pl.when(holder == core)
+    def _():
+        zall[b, c] = own[...]
 
     def ag_copy(dest, origin):
         return pltpu.make_async_remote_copy(
-            src_ref=zall.at[b, origin], dst_ref=zall.at[b, origin],
-            send_sem=ag_send.at[dest], recv_sem=ag_recv.at[origin],
+            src_ref=own, dst_ref=zall.at[b, origin],
+            send_sem=ag_send.at[dest // 2], recv_sem=ag_recv.at[origin],
             device_id=(dest, b), device_id_type=MESH)
 
+    def ag_dest(i):
+        return 2 * lax.rem(c // 2 + i, half) + holder
+
     def ag_start(i, carry):
-        ag_copy(lax.rem(c + i, chans), c).start()
-        return carry
-
-    lax.fori_loop(1, chans, ag_start, 0)
+        dest = ag_dest(i)
+
+        @pl.when(dest != c)
+        def _():
+            ag_copy(dest, c).start()
+        return carry
+
+    lax.fori_loop(0, half, ag_start, 0)
 
     def a2a_copy(dest, origin):
         return pltpu.make_async_remote_copy(
@@ -188,8 +202,6 @@
 
         lax.fori_loop(0, number, one, 0)
 
-    core = lax.rem(c, 2)
-    twin = c + 1 - 2 * core
     right = lax.rem(b + 1, bands)
     left = lax.rem(b + bands - 1, bands)
 
@@ -209,29 +221,29 @@
             src_ref=ref, dst_ref=ref, send_sem=sems[0].at[piece, step - 1], recv_sem=sems[1].at[piece, step - 1],
             device_id=(c, right if way > 0 else left), device_id_type=MESH)
 
-    def share(piece, step, way, own):
+    def share(piece, step, way, mine):
         origin = lax.rem(b + bands - way * step, bands)
-        ref = part(origin, core if own else 1 - core, piece, step, way)
-        k = 2 * (step - 1) + (0 if way > 0 else 1)
+        ref = part(origin, core if mine else 1 - core, piece, step, way)
+        k = 2 * step - (1 if way > 0 else 0) if step else 0
         return pltpu.make_async_remote_copy(
             src_ref=ref, dst_ref=ref, send_sem=sib_send.at[piece, k], recv_sem=sib_recv.at[piece, k],
             device_id=(twin, b), device_id_type=MESH)
 
+    def begin(piece):
+        ag_wait(half * core + size * piece, size)
+        for way in (1, -1):
+            hop(piece, 1, way, 0).start()
+        share(piece, 0, 1, True).start()
+
     def advance(piece, step):
-        if step == 1:
-            ag_wait(half * core + size * piece, size)
-        else:
-            for way in (1, -1):
-                hop(piece, step - 1, way, 1).wait_recv()
-        if step <= last:
-            for way in (1, -1):
+        for way in (1, -1):
+            hop(piece, step - 1, way, 1).wait_recv()
+            if step <= last:
                 hop(piece, step, way, 0).start()
-        if step > 1:
-            for way in (1, -1):
-                share(piece, step - 1, way, True).start()
+            share(piece, step - 1, way, True).start()
 
     def arrived(piece):
-        ag_wait(half * (1 - core) + size * piece, size)
+        share(piece, 0, 1, False).wait_recv()
         for step in range(1, last + 1):
             for way in (1, -1):
                 share(piece, step, way, False).wait_recv()
@@ -272,27 +284,15 @@
 
         lax.fori_loop(0, size // 2, pair, 0)
 
-    first = list(range((pieces + 1) // 2))
-    second = list(range((pieces + 1) // 2, pieces))
-    for step in range(1, last + 1):
-        for piece in first:
+    for piece in range(pieces):
+        begin(piece)
+    for step in range(2, last + 2):
+        for piece in range(pieces):
             advance(piece, step)
-    for piece in second:
-        advance(piece, 1)
-    for piece in first:
-        advance(piece, last + 1)
-    for piece in first:
+    for piece in range(pieces):
         arrived(piece)
-    work = [(owner, piece) for piece in first for owner in range(2)]
-    for step in range(2, last + 2):
-        if work and second:
-            stack_piece(*work.pop(0))
-        for piece in second:
-            advance(piece, step)
-    for piece in second:
-        arrived(piece)
-    for owner, piece in work + [(owner, piece) for piece in second for owner in range(2)]:
-        stack_piece(owner, piece)
+        for owner in range(2):
+            stack_piece(owner, piece)
 
     def out_copy(g):
         return pltpu.make_async_copy(turned.at[g], cross_out.at[g], out_sem.at[g])
@@ -317,12 +317,21 @@
     def chan_done(i, carry):
         other = lax.rem(c + i, chans)
         a2a_copy(other, c).wait_send()
-        ag_copy(other, c).wait_send()
+        return carry
+
+    def ag_done(i, carry):
+        dest = ag_dest(i)
+
+        @pl.when(dest != c)
+        def _():
+            ag_copy(dest, c).wait_send()
         return carry
 
     lax.fori_loop(1, bands, rs_done, 0)
     lax.fori_loop(1, chans, chan_done, 0)
+    lax.fori_loop(0, half, ag_done, 0)
     for piece in range(pieces):
+        share(piece, 0, 1, True).wait_send()
         for step in range(1, last + 1):
             for way in (1, -1):
                 hop(piece, step, way, 0).wait_send()
@@ -368,14 +377,15 @@
             pltpu.VMEM((chans, 2 * RX, depth), bf16),
             pltpu.VMEM((chans, 2 * RX, depth), bf16),
             pltpu.VMEM((bands, rows, 128), bf16),
+            pltpu.VMEM((rows, 128), bf16),
             pltpu.VMEM((bands, chans, rows, 128), bf16),
             pltpu.VMEM((2, 2 * RX, depth), f32),
             pltpu.VMEM((2, RX, bins // 2, 128), f32),
             pltpu.VMEM((RX // 8, 8, SRC, 2 * bins), bf16),
             pltpu.VMEM((2, bins, LAGS // 2), bf16),
-            dma((chans,)), dma((chans,)), dma((bands,)), dma((bands,)), dma((chans,)), dma((chans,)),
+            dma((chans,)), dma((chans,)), dma((bands,)), dma((bands,)), dma((chans // 2,)), dma((chans,)),
             dma((pieces, last)), dma((pieces, last)), dma((pieces, last)), dma((pieces, last)),
-            dma((pieces, 2 * last)), dma((pieces, 2 * last)), dma((RX // 8 + 1,)),
+            dma((pieces, 2 * last + 1)), dma((pieces, 2 * last + 1)), dma((RX // 8 + 1,)),
         ],
         compiler_params=pltpu.CompilerParams(
             collective_id=tiles, has_side_effects=True, vmem_limit_bytes=48 * 1024 * 1024

time: 80.9 us -> 71.9 us (0.89)
  Pallas kernels: 76.8 us -> 68.4 us
    pallas_call x1, Pallas kernels: 65.7 us -> 57.3 us  [stacked(): pl.pallas_call(functools.partial(stack_kernel, tiles, chans, bands), out_...]
where the time goes in v3:
time: 71.9 us; the launch traced here: 71.3 us
  Pallas kernels  68.4 us (95%)
  between operations  1.31 us (2%)
  other arithmetic  1.29 us (2%)
    pallas_call x1, Pallas kernels, stacked(): pl.pallas_call(functools.partial(stack_kernel, tiles, chans, bands), out_...  57.3 us
    pallas_call x1, Pallas kernels, correlate(): pl.pallas_call(lag_kernel, grid=(RX // 8,), out_shape=jax.ShapeDtypeStruc...  8.41 us
    pallas_call x1, Pallas kernels, stacked(): pl.pallas_call(functools.partial(pack_kernel, tiles, chans, bands), out_s...  2.7 us

profile of v3, /device:TPU:1, one launch (start us, length us, event | category | flops | bytes accessed | tf_op | source)
XLA Modules:
  0.0 71.3 jit_solution(2986767271843645128)
XLA Ops:
  0.0 1.3 %reduce_sum.9 = s32[]{:T(128)} reduce(s32[30]{0:T(128)} %param.8, s32[]{:T(128)} %constant.4.clone.1), dimensions={0}, to_apply=%region_0.0 | reduce | flops 29 | bytes 128 | tf_op jit(solution)/shard_map/reduce_sum | solution.py:431
  2.6 60.2 %conditional.1 = ((bf16[4,8,64,1024]{3,2,1,0:T(8,128)(2,1)}, bf16[2,512,512]{2,1,0:T(8,128)(2,1)S(1)})) conditional(s32[]{:T(128)} %clamp.3, (s32[1]{0:T(128)}, s32[30]{0:T(128)}, bf16[2,30,16,1024]{3,2,1,0:T(8,128)(2,1)}) %tuple.14, (s32[1]{0:T(128)}, s32[30]{0:T(128)}, bf16[2,30,16,1024]{3,2,1,0:T(8,128)(2,1)}) %tuple.14, ...), branch_computations={%region_1.0_spmd, %region_2.0_spmd, %region_3.0_spmd} | conditional | flops 4294967296 | bytes 8388636 | solution.py:433
  2.6 2.7 %branch_0_fun.2 = (bf16[2,256,1024]{2,1,0:T(8,128)(2,1)S(1)}, bf16[8,32,128]{2,1,0:T(8,128)(2,1)S(1)}, f32[8,128]{1,0:T(8,128)S(1)}) custom-call(s32[1]{0:T(128)} %bitcast.band_ref, s32[1]{0:T(128)} %get-tuple-element.23.block_ref, s32[30]{0:T(128)} %get-tuple-element.24.flags_ref, bf16[2,30,16,1024]{3,2,1,0:T(8,128)(2,1)} %get-tuple-element.25.x_ref), custom_call_target="tpu_custom_call" | custom-call | tf_op jit(solution)/shard_map/cond/branch_0_fun/pallas_call | solution.py:355
  5.3 57.3 %branch_0_fun.3 = (bf16[4,8,64,1024]{3,2,1,0:T(8,128)(2,1)}, bf16[2,512,512]{2,1,0:T(8,128)(2,1)S(1)}) custom-call(bf16[2,256,1024]{2,1,0:T(8,128)(2,1)S(1)} %get-tuple-element.26.xs, bf16[8,32,128]{2,1,0:T(8,128)(2,1)S(1)} %get-tuple-element.27.cand, f32[8,128]{1,0:T(8,128)S(1)} %get-tuple-element.28.scale_ref), custom_call_target="tpu_custom_call" | custom-call | flops 2147483648 | bytes 8388608 | tf_op jit(solution)/shard_map/cond/branch_0_fun/pallas_call | solution.py:368
  62.8 8.4 %shard_map.37 = f32[64,1,32,1024]{3,2,1,0:T(8,128)} custom-call(bf16[4,8,64,1024]{3,2,1,0:T(8,128)(2,1)} %get-tuple-element.43.cross_ref, bf16[2,512,512]{2,1,0:T(8,128)(2,1)S(1)} %get-tuple-element.44.weights_ref), custom_call_target="tpu_custom_call" | custom-call | flops 2147483648 | bytes 16777216 | tf_op jit(solution)/shard_map/pallas_call | solution.py:411

commit v4 on v3

--- a/solution.py
+++ b/solution.py
@@ -10,6 +10,7 @@
 
 LAGS = 1024
 SEG = 30
+SLOTS = 32
 SRC = 64
 BINS = 16
 RX = 32
@@ -35,10 +36,8 @@
     return cos_part.astype(jnp.bfloat16), sin_part.astype(jnp.bfloat16)
 
 
-def pack_kernel(tiles, chans, bands, band_ref, block_ref, flags_ref, x_ref, xs_ref, cand_ref, scale_ref, following):
-    segs = 8 * tiles
-    depth = BINS * segs
-    rows = depth // bands
+def pack_kernel(chans, band_ref, block_ref, flags_ref, x_ref, xs_ref, cand_ref, scale_ref, tier_ref, following):
+    depth = BINS * SLOTS
     f32, bf16 = jnp.float32, jnp.bfloat16
 
     following[SEG] = SEG
@@ -57,7 +56,9 @@
         xs_ref[1, place, :] = x_ref[1, g]
         return following[jnp.minimum(at + 1, SEG)]
 
-    lax.fori_loop(0, segs, pack, following[0])
+    tier = jnp.maximum((valid + 7) // 8 - 2, 0)
+    tier_ref[0] = tier
+    lax.fori_loop(0, 8 * (tier + 2), pack, following[0])
 
     first = block_ref[0] * SRC
     width = RX * chans
@@ -74,18 +75,19 @@
     mine = jnp.where(upper == 0, low, high)
     count = jnp.where(owner == band_ref[0], valid, 0)
     mine = jnp.where(slot < count, mine, 0.0).astype(bf16)
-    cand_ref[...] = mine.reshape(bands, rows, 128)
+    cand_ref[...] = mine
     scale_ref[...] = 1.0 / jnp.full((8, 128), valid, jnp.int32).astype(f32)
 
 
 def stack_kernel(
     tiles, chans, bands,
-    xs, cand, scale_ref, cross_out, table_out,
-    send, recv, parts, own, zall, spread, cross, turned, table,
+    xs, cand, scale_ref, turned, table,
+    send, recv, parts, own, zall, spread, cross,
     a2a_send, a2a_recv, rs_send, rs_recv, ag_send, ag_recv,
-    right_send, right_recv, left_send, left_recv, sib_send, sib_recv, out_sem,
+    right_send, right_recv, left_send, left_recv, sib_send, sib_recv,
 ):
     depth = BINS * 8 * tiles
+    rows = depth // bands
     bins = BINS * chans
     half = chans // 2
     pieces = max(1, half // 4)
@@ -112,9 +114,9 @@
     def turn(block, carry):
         lanes = pl.ds(pl.multiple_of(block * 128, 128), 128)
         for comp in range(2):
-            rows = xs[comp, :, lanes].T
+            lines = xs[comp, :depth, lanes].T
             for q in range(4):
-                send[4 * block + q, comp * RX:(comp + 1) * RX, :] = rows[q * RX:(q + 1) * RX]
+                send[4 * block + q, comp * RX:(comp + 1) * RX, :] = lines[q * RX:(q + 1) * RX]
         return carry
 
     lax.fori_loop(0, groups, turn, 0)
@@ -124,7 +126,7 @@
 
     def rs_copy(other, slot):
         return pltpu.make_async_remote_copy(
-            src_ref=cand.at[other], dst_ref=parts.at[slot],
+            src_ref=cand.at[pl.ds(pl.multiple_of(other * rows, rows), rows)], dst_ref=parts.at[slot],
             send_sem=rs_send.at[other], recv_sem=rs_recv.at[slot],
             device_id=(c, other), device_id_type=MESH)
 
@@ -145,8 +147,6 @@
         return carry
 
     lax.fori_loop(0, bins // 2 // count, fill, 0)
-    table_copy = pltpu.make_async_copy(table, table_out, out_sem.at[RX // 8])
-    table_copy.start()
 
     def rs_sum(i, total):
         other = lax.rem(b + i, bands)
@@ -156,7 +156,7 @@
     core = lax.rem(c, 2)
     twin = c + 1 - 2 * core
     holder = c // half
-    own[...] = lax.fori_loop(1, bands, rs_sum, cand[b].astype(f32)).astype(bf16)
+    own[...] = lax.fori_loop(1, bands, rs_sum, cand[pl.ds(pl.multiple_of(b * rows, rows), rows), :].astype(f32)).astype(bf16)
 
     @pl.when(holder == core)
     def _():
@@ -255,9 +255,6 @@
     sign = jnp.where(lax.broadcasted_iota(jnp.int32, (1, 128), 1) < SRC, 1.0, -1.0)
 
     def stack(j, buffer):
-        @pl.when(j != c)
-        def _():
-            a2a_copy(j, j).wait_recv()
         z = zall[:, j].reshape(depth, 128)
         swapped = (pltpu.roll(z.astype(f32), SRC, 1) * sign).astype(bf16)
         weights = jnp.concatenate([z, swapped], axis=0)
@@ -277,25 +274,44 @@
             cross[1, 8 * g:8 * g + 8, place, :] = product[:, BINS // 2:]
 
     def stack_piece(owner, piece):
-        def pair(i, carry):
-            for k in range(2):
-                stack(half * owner + size * piece + 2 * i + k, k)
+        start = half * owner + size * piece
+
+        def a2a_wait(i, carry):
+            @pl.when(start + i != c)
+            def _():
+                a2a_copy(start + i, start + i).wait_recv()
             return carry
 
-        lax.fori_loop(0, size // 2, pair, 0)
+        lax.fori_loop(0, size, a2a_wait, 0)
+        for k in range(size):
+            stack(start + k, k)
+
+    def finish(piece):
+        arrived(piece)
+
+        def both(owner, carry):
+            stack_piece(owner, piece)
+            return carry
+
+        lax.fori_loop(0, 2, both, 0)
 
     for piece in range(pieces):
         begin(piece)
-    for step in range(2, last + 2):
+    if pieces == 4 and last == 4:
+        order = [(0, 2), (1, 2), (2, 2), (0, 3), (1, 3), (3, 2), (0, 4), (1, 4), (2, 3), (3, 3), (0, 5), (1, 5), (2, 4), (3, 4)]
+        for piece, step in order:
+            advance(piece, step)
+        finish(0)
+        advance(2, 5)
+        advance(3, 5)
+        for piece in range(1, pieces):
+            finish(piece)
+    else:
+        for step in range(2, last + 2):
+            for piece in range(pieces):
+                advance(piece, step)
         for piece in range(pieces):
-            advance(piece, step)
-    for piece in range(pieces):
-        arrived(piece)
-        for owner in range(2):
-            stack_piece(owner, piece)
-
-    def out_copy(g):
-        return pltpu.make_async_copy(turned.at[g], cross_out.at[g], out_sem.at[g])
+            finish(piece)
 
     k = bins // 2
     for g in range(RX // 8):
@@ -303,12 +319,11 @@
             for r in (2 * i, 2 * i + 1):
                 for parity in range(2):
                     flat = cross[parity, 8 * g + r].astype(bf16).T
-                    turned[g, r, :, 2 * parity * k:(2 * parity + 1) * k] = flat[:SRC]
-                    turned[g, r, :, (2 * parity + 1) * k:(2 * parity + 2) * k] = flat[SRC:]
+                    turned[8 * g + r, :, 2 * parity * k:(2 * parity + 1) * k] = flat[:SRC]
+                    turned[8 * g + r, :, (2 * parity + 1) * k:(2 * parity + 2) * k] = flat[SRC:]
             return carry
 
         lax.fori_loop(0, 4, turn_back, 0)
-        out_copy(g).start()
 
     def rs_done(i, carry):
         rs_copy(lax.rem(b + i, bands), b).wait_send()
@@ -336,87 +351,87 @@
             for way in (1, -1):
                 hop(piece, step, way, 0).wait_send()
                 share(piece, step, way, True).wait_send()
-    table_copy.wait()
-    for g in range(RX // 8):
-        out_copy(g).wait()
-
-
-def stacked(tiles, chans, bands, block, flags, x):
+
+
+def packed(chans, block, flags, x):
+    vmem = pl.BlockSpec(memory_space=pltpu.VMEM)
+    smem = pl.BlockSpec(memory_space=pltpu.SMEM)
+    depth = BINS * SLOTS
+    return pl.pallas_call(
+        functools.partial(pack_kernel, chans),
+        out_shape=(
+            jax.ShapeDtypeStruct((2, depth, RX * chans), jnp.bfloat16),
+            jax.ShapeDtypeStruct((depth, 128), jnp.bfloat16),
+            jax.ShapeDtypeStruct((8, 128), jnp.float32),
+            jax.ShapeDtypeStruct((1,), jnp.int32),
+        ),
+        in_specs=[smem, smem, smem, vmem],
+        out_specs=(vmem, vmem, vmem, smem),
+        scratch_shapes=[pltpu.SMEM((SLOTS,), jnp.int32)],
+        compiler_params=pltpu.CompilerParams(vmem_limit_bytes=24 * 1024 * 1024),
+    )(lax.axis_index("band").reshape(1), block, flags, x)
+
+
+def stacked(tiles, chans, bands, xs, cand, scale):
     depth = BINS * 8 * tiles
     rows = depth // bands
     bins = BINS * chans
     pieces = max(1, chans // 8)
+    size = chans // 2 // pieces
     last = bands // 2
     dma = pltpu.SemaphoreType.DMA
     f32, bf16 = jnp.float32, jnp.bfloat16
     vmem = pl.BlockSpec(memory_space=pltpu.VMEM)
-    smem = pl.BlockSpec(memory_space=pltpu.SMEM)
-    hbm = pl.BlockSpec(memory_space=pl.ANY)
-    packed = pl.pallas_call(
-        functools.partial(pack_kernel, tiles, chans, bands),
-        out_shape=(
-            jax.ShapeDtypeStruct((2, depth, RX * chans), bf16),
-            jax.ShapeDtypeStruct((bands, rows, 128), bf16),
-            jax.ShapeDtypeStruct((8, 128), f32),
-        ),
-        in_specs=[smem, smem, smem, vmem],
-        out_specs=(vmem, vmem, vmem),
-        scratch_shapes=[pltpu.SMEM((32,), jnp.int32)],
-        compiler_params=pltpu.CompilerParams(vmem_limit_bytes=24 * 1024 * 1024),
-    )(lax.axis_index("band").reshape(1), block, flags, x)
     flops = 2 * chans * RX * BINS * 2 * depth * 128
     return pl.pallas_call(
         functools.partial(stack_kernel, tiles, chans, bands),
         out_shape=(
-            jax.ShapeDtypeStruct((RX // 8, 8, SRC, 2 * bins), bf16),
+            jax.ShapeDtypeStruct((RX, SRC, 2 * bins), bf16),
             jax.ShapeDtypeStruct((2, bins, LAGS // 2), bf16),
         ),
         in_specs=[vmem] * 3,
-        out_specs=(hbm, hbm),
+        out_specs=(vmem, vmem),
         scratch_shapes=[
             pltpu.VMEM((chans, 2 * RX, depth), bf16),
             pltpu.VMEM((chans, 2 * RX, depth), bf16),
             pltpu.VMEM((bands, rows, 128), bf16),
             pltpu.VMEM((rows, 128), bf16),
             pltpu.VMEM((bands, chans, rows, 128), bf16),
-            pltpu.VMEM((2, 2 * RX, depth), f32),
+            pltpu.VMEM((size, 2 * RX, depth), f32),
             pltpu.VMEM((2, RX, bins // 2, 128), f32),
-            pltpu.VMEM((RX // 8, 8, SRC, 2 * bins), bf16),
-            pltpu.VMEM((2, bins, LAGS // 2), bf16),
             dma((chans,)), dma((chans,)), dma((bands,)), dma((bands,)), dma((chans // 2,)), dma((chans,)),
             dma((pieces, last)), dma((pieces, last)), dma((pieces, last)), dma((pieces, last)),
-            dma((pieces, 2 * last + 1)), dma((pieces, 2 * last + 1)), dma((RX // 8 + 1,)),
+            dma((pieces, 2 * last + 1)), dma((pieces, 2 * last + 1)),
         ],
         compiler_params=pltpu.CompilerParams(
-            collective_id=tiles, has_side_effects=True, vmem_limit_bytes=48 * 1024 * 1024
+            collective_id=tiles, has_side_effects=True, vmem_limit_bytes=36 * 1024 * 1024
         ),
         cost_estimate=pl.CostEstimate(flops=flops, bytes_accessed=8 * 1024 * 1024, transcendentals=0),
-    )(*packed)
+    )(xs, cand, scale)
 
 
 def lag_kernel(cross_ref, weights_ref, out_ref):
     k = weights_ref.shape[1]
-    left = cross_ref[0].reshape(8 * SRC, 2 * k)
-    even = jnp.dot(left[:, :k], weights_ref[0], preferred_element_type=jnp.float32)
-    odd = jnp.dot(left[:, k:], weights_ref[1], preferred_element_type=jnp.float32)
-    low = (even + odd).reshape(8, SRC, LAGS // 2)
-    high = (even - odd).reshape(8, SRC, LAGS // 2)
-    for r in range(8):
-        out_ref[:, 0, r, :LAGS // 2] = low[r]
-        out_ref[:, 0, r, LAGS // 2:] = high[r]
+    for q in range(SRC // BINS):
+        sources = slice(BINS * q, BINS * q + BINS)
+        left = cross_ref[:, sources, :].reshape(RX * BINS, 2 * k)
+        even = jnp.dot(left[:, :k], weights_ref[0], preferred_element_type=jnp.float32)
+        odd = jnp.dot(left[:, k:], weights_ref[1], preferred_element_type=jnp.float32)
+        low = (even + odd).reshape(RX, BINS, LAGS // 2)
+        high = (even - odd).reshape(RX, BINS, LAGS // 2)
+        for r in range(RX):
+            out_ref[sources, 0, r, :LAGS // 2] = low[r]
+            out_ref[sources, 0, r, LAGS // 2:] = high[r]
 
 
 def correlate(cross, weights):
     k = weights.shape[1]
+    vmem = pl.BlockSpec(memory_space=pltpu.VMEM)
     return pl.pallas_call(
         lag_kernel,
-        grid=(RX // 8,),
         out_shape=jax.ShapeDtypeStruct((SRC, 1, RX, LAGS), jnp.float32),
-        in_specs=[
-            pl.BlockSpec((1, 8, SRC, 2 * k), lambda i: (i, 0, 0, 0)),
-            pl.BlockSpec((2, k, LAGS // 2), lambda i: (0, 0, 0)),
-        ],
-        out_specs=pl.BlockSpec((SRC, 1, 8, LAGS), lambda i: (0, 0, i, 0)),
+        in_specs=[vmem] * 2,
+        out_specs=vmem,
         compiler_params=pltpu.CompilerParams(vmem_limit_bytes=32 * 1024 * 1024),
         cost_estimate=pl.CostEstimate(
             flops=2 * SRC * RX * k * LAGS, bytes_accessed=16 * 1024 * 1024, transcendentals=0
@@ -428,14 +443,12 @@
     chans, bands = mesh.shape["chan"], mesh.shape["band"]
 
     def local(spectra, source_block, segment_flags):
-        valid = jnp.sum(segment_flags)
-        tier = (valid > 16).astype(jnp.int32) + (valid > 24).astype(jnp.int32)
-        cross, weights = lax.switch(
-            tier,
-            [functools.partial(stacked, tiles, chans, bands) for tiles in (2, 3, 4)],
-            source_block, segment_flags, spectra,
-        )
-        return correlate(cross, weights)
+        *operands, tier = packed(chans, source_block, segment_flags, spectra)
+
+        def branch(tiles):
+            return lambda *arrays: correlate(*stacked(tiles, chans, bands, *arrays))
+
+        return lax.switch(tier[0], [branch(tiles) for tiles in (2, 3, 4)], *operands)
 
     return jax.shard_map(
         local,

time: 71.9 us -> 75.4 us (1.049)
  local copies, waits for them, and re-layouts: 0 us -> 5.58 us
  Pallas kernels: 68.4 us -> 66.7 us
  other arithmetic: 1.29 us -> 0 us
    unnamed x0 -> x6, local copies, waits for them, and re-layouts: none -> 5.58 us
    pallas_call x2, Pallas kernels: 11.1 us -> 6.04 us  [the longest x1 4.53 us: correlate(): pl.pallas_call(lag_kernel, out_shape=jax.ShapeDtypeStruct((SRC, 1, RX, LA...]
    pallas_call x1, Pallas kernels: 57.3 us -> 60.7 us  [stacked(): pl.pallas_call(functools.partial(stack_kernel, tiles, chans, bands), out_...]
    reduce_sum x1 -> x0, other arithmetic: 1.29 us -> none  [local(): valid = jnp.sum(segment_flags)]
where the time goes in v4:
time: 75.4 us; the launch traced here: 74.2 us
  Pallas kernels  66.7 us (88%)
  local copies, waits for them, and re-layouts  5.58 us (7%)
  between operations  1.37 us (2%)
    pallas_call x1, Pallas kernels, stacked(): pl.pallas_call(functools.partial(stack_kernel, tiles, chans, bands), out_...  60.7 us
    unnamed x6, local copies, waits for them, and re-layouts  5.58 us
    pallas_call x1, Pallas kernels, correlate(): pl.pallas_call(lag_kernel, out_shape=jax.ShapeDtypeStruct((SRC, 1, RX, LA...  4.53 us

profile of v4, /device:TPU:1, one launch (start us, length us, event | category | flops | bytes accessed | tf_op | source)
XLA Modules:
  0.0 74.2 jit_solution(5557494837882073557)
XLA Ops:
  0.7 0.0 copy-start
  0.7 1.5 %copy-done = bf16[2,30,16,1024]{3,2,1,0:T(8,128)(2,1)S(1)} copy-done((bf16[2,30,16,1024]{3,2,1,0:T(8,128)(2,1)S(1)}, bf16[2,30,16,1024]{3,2,1,0:T(8,128)(2,1)}, u32[]{:S(2)}) %copy-start) | copy-done | bytes 1966104
  2.2 0.0 copy-start.1
  2.2 0.7 copy-done.1
  2.9 1.5 %shard_map.40 = (bf16[2,512,1024]{2,1,0:T(8,128)(2,1)S(1)}, bf16[512,128]{1,0:T(8,128)(2,1)S(1)}, f32[8,128]{1,0:T(8,128)S(1)}, s32[1]{0:T(128)}) custom-call(s32[1]{0:T(128)} %bitcast.band_ref, s32[1]{0:T(128)S(6)} %copy.10.block_ref, s32[30]{0:T(128)S(1)} %copy-done.1, bf16[2,30,16,1024]{3,2,1,0:T(8,128)(2,1)S(1)} %copy-done), custom_call_target="tpu_custom_call" | custom-call | tf_op jit(solution)/shard_map/pallas_call | solution.py:360
  5.0 65.7 %conditional.1 = (f32[64,1,32,1024]{3,2,1,0:T(8,128)S(1)}) conditional(s32[]{:T(128)} %bitcast.1, (bf16[2,512,1024]{2,1,0:T(8,128)(2,1)S(1)}, bf16[512,128]{1,0:T(8,128)(2,1)S(1)}, f32[8,128]{1,0:T(8,128)S(1)}) %tuple.14, (bf16[2,512,1024]{2,1,0:T(8,128)(2,1)S(1)}, bf16[512,128]{1,0:T(8,128)(2,1)S(1)}, ...), branch_computations={%region_0.0_spmd, %region_1.0_spmd, %region_2.0_spmd} | conditional | flops 6442450944 | bytes 25165832 | solution.py:451
  5.1 60.7 %branch_1_fun.2 = (bf16[32,64,1024]{2,1,0:T(8,128)(2,1)S(1)}, bf16[2,512,512]{2,1,0:T(8,128)(2,1)S(1)}) custom-call(bf16[2,512,1024]{2,1,0:T(8,128)(2,1)S(1)} %get-tuple-element.32.xs, bf16[512,128]{1,0:T(8,128)(2,1)S(1)} %get-tuple-element.33.cand, f32[8,128]{1,0:T(8,128)S(1)} %get-tuple-element.34.scale_ref), custom_call_target="tpu_custom_call" | custom-call | flops 3221225472 | bytes 8388608 | tf_op jit(solution)/shard_map/cond/branch_1_fun/pallas_call | solution.py:386
  65.8 4.5 %branch_1_fun.3 = f32[64,1,32,1024]{3,2,1,0:T(8,128)S(1)} custom-call(bf16[32,64,1024]{2,1,0:T(8,128)(2,1)S(1)} %get-tuple-element.35.cross_ref, bf16[2,512,512]{2,1,0:T(8,128)(2,1)S(1)} %get-tuple-element.36.weights_ref), custom_call_target="tpu_custom_call" | custom-call | flops 2147483648 | bytes 16777216 | tf_op jit(solution)/shard_map/cond/branch_1_fun/pallas_call | solution.py:430
  70.8 0.0 copy-start.2
  70.8 3.4 %copy-done.2 = f32[64,1,32,1024]{3,2,1,0:T(8,128)} copy-done((f32[64,1,32,1024]{3,2,1,0:T(8,128)}, f32[64,1,32,1024]{3,2,1,0:T(8,128)S(1)}, u32[]{:S(2)}) %copy-start.2) | copy-done | bytes 8388632
Async XLA Ops:
  0.7 1.5 %copy-start = (bf16[2,30,16,1024]{3,2,1,0:T(8,128)(2,1)S(1)}, bf16[2,30,16,1024]{3,2,1,0:T(8,128)(2,1)}, u32[]{:S(2)}) copy-start(bf16[2,30,16,1024]{3,2,1,0:T(8,128)(2,1)} %x_ref.1) | copy-start | bytes 5898244
  2.2 0.7 copy-start.1
  70.8 3.4 %copy-start.2 = (f32[64,1,32,1024]{3,2,1,0:T(8,128)}, f32[64,1,32,1024]{3,2,1,0:T(8,128)S(1)}, u32[]{:S(2)}) copy-start(f32[64,1,32,1024]{3,2,1,0:T(8,128)S(1)} %get-tuple-element.54) | copy-start | bytes 25165828

commit v5 on v4

--- a/solution.py
+++ b/solution.py
@@ -90,7 +90,7 @@
     rows = depth // bands
     bins = BINS * chans
     half = chans // 2
-    pieces = max(1, half // 4)
+    pieces = max(1, half // 8)
     size = half // pieces
     last = bands // 2
     groups = chans // 4
@@ -190,8 +190,6 @@
     def a2a_start(i, carry):
         a2a_copy(lax.rem(c + i, chans), c).start()
         return carry
-
-    lax.fori_loop(1, chans, a2a_start, 0)
 
     def ag_wait(start, number):
         def one(i, carry):
@@ -274,17 +272,23 @@
             cross[1, 8 * g:8 * g + 8, place, :] = product[:, BINS // 2:]
 
     def stack_piece(owner, piece):
-        start = half * owner + size * piece
-
-        def a2a_wait(i, carry):
-            @pl.when(start + i != c)
-            def _():
-                a2a_copy(start + i, start + i).wait_recv()
+        few = min(size, 4)
+
+        def group(g, carry):
+            start = half * owner + size * piece + few * g
+
+            def a2a_wait(i, inner):
+                @pl.when(start + i != c)
+                def _():
+                    a2a_copy(start + i, start + i).wait_recv()
+                return inner
+
+            lax.fori_loop(0, few, a2a_wait, 0)
+            for k in range(few):
+                stack(start + k, k)
             return carry
 
-        lax.fori_loop(0, size, a2a_wait, 0)
-        for k in range(size):
-            stack(start + k, k)
+        lax.fori_loop(0, size // few, group, 0)
 
     def finish(piece):
         arrived(piece)
@@ -297,21 +301,12 @@
 
     for piece in range(pieces):
         begin(piece)
-    if pieces == 4 and last == 4:
-        order = [(0, 2), (1, 2), (2, 2), (0, 3), (1, 3), (3, 2), (0, 4), (1, 4), (2, 3), (3, 3), (0, 5), (1, 5), (2, 4), (3, 4)]
-        for piece, step in order:
+    lax.fori_loop(1, chans, a2a_start, 0)
+    for step in range(2, last + 2):
+        for piece in range(pieces):
             advance(piece, step)
-        finish(0)
-        advance(2, 5)
-        advance(3, 5)
-        for piece in range(1, pieces):
-            finish(piece)
-    else:
-        for step in range(2, last + 2):
-            for piece in range(pieces):
-                advance(piece, step)
-        for piece in range(pieces):
-            finish(piece)
+    for piece in range(pieces):
+        finish(piece)
 
     k = bins // 2
     for g in range(RX // 8):
@@ -376,8 +371,7 @@
     depth = BINS * 8 * tiles
     rows = depth // bands
     bins = BINS * chans
-    pieces = max(1, chans // 8)
-    size = chans // 2 // pieces
+    pieces = max(1, chans // 16)
     last = bands // 2
     dma = pltpu.SemaphoreType.DMA
     f32, bf16 = jnp.float32, jnp.bfloat16
@@ -397,7 +391,7 @@
             pltpu.VMEM((bands, rows, 128), bf16),
             pltpu.VMEM((rows, 128), bf16),
             pltpu.VMEM((bands, chans, rows, 128), bf16),
-            pltpu.VMEM((size, 2 * RX, depth), f32),
+            pltpu.VMEM((4, 2 * RX, depth), f32),
             pltpu.VMEM((2, RX, bins // 2, 128), f32),
             dma((chans,)), dma((chans,)), dma((bands,)), dma((bands,)), dma((chans // 2,)), dma((chans,)),
             dma((pieces, last)), dma((pieces, last)), dma((pieces, last)), dma((pieces, last)),

time: 75.4 us -> 71.6 us (0.950); the launches traced: 74.2 us -> 71.5 us
  Pallas kernels: 66.7 us -> 64 us
    pallas_call x1, Pallas kernels: 60.7 us -> 58 us  [stacked(): pl.pallas_call(functools.partial(stack_kernel, tiles, chans, bands), out_...]
where the time goes in v5:
time: 71.6 us; the launch traced here: 71.5 us
  Pallas kernels  64 us (89%)
  local copies, waits for them, and re-layouts  5.58 us (8%)
  between operations  1.37 us (2%)
    pallas_call x1, Pallas kernels, stacked(): pl.pallas_call(functools.partial(stack_kernel, tiles, chans, bands), out_...  58 us
    unnamed x6, local copies, waits for them, and re-layouts  5.58 us
    pallas_call x1, Pallas kernels, correlate(): pl.pallas_call(lag_kernel, out_shape=jax.ShapeDtypeStruct((SRC, 1, RX, LA...  4.53 us
    pallas_call x1, Pallas kernels, packed(): pl.pallas_call(functools.partial(pack_kernel, chans), out_shape=(jax.Shap...  1.5 us

profile of v5, /device:TPU:1, one launch (start us, length us, event | category | flops | bytes accessed | tf_op | source)
XLA Modules:
  0.0 71.5 jit_solution(5728200811425057429)
XLA Ops:
  0.7 0.0 copy-start
  0.7 1.5 %copy-done = bf16[2,30,16,1024]{3,2,1,0:T(8,128)(2,1)S(1)} copy-done((bf16[2,30,16,1024]{3,2,1,0:T(8,128)(2,1)S(1)}, bf16[2,30,16,1024]{3,2,1,0:T(8,128)(2,1)}, u32[]{:S(2)}) %copy-start) | copy-done | bytes 1966104
  2.2 0.0 copy-start.1
  2.2 0.7 copy-done.1
  2.9 1.5 %shard_map.40 = (bf16[2,512,1024]{2,1,0:T(8,128)(2,1)S(1)}, bf16[512,128]{1,0:T(8,128)(2,1)S(1)}, f32[8,128]{1,0:T(8,128)S(1)}, s32[1]{0:T(128)}) custom-call(s32[1]{0:T(128)} %bitcast.band_ref, s32[1]{0:T(128)S(6)} %copy.10.block_ref, s32[30]{0:T(128)S(1)} %copy-done.1, bf16[2,30,16,1024]{3,2,1,0:T(8,128)(2,1)S(1)} %copy-done), custom_call_target="tpu_custom_call" | custom-call | tf_op jit(solution)/shard_map/pallas_call | solution.py:355
  5.0 63.1 %conditional.1 = (f32[64,1,32,1024]{3,2,1,0:T(8,128)S(1)}) conditional(s32[]{:T(128)} %bitcast.1, (bf16[2,512,1024]{2,1,0:T(8,128)(2,1)S(1)}, bf16[512,128]{1,0:T(8,128)(2,1)S(1)}, f32[8,128]{1,0:T(8,128)S(1)}) %tuple.14, (bf16[2,512,1024]{2,1,0:T(8,128)(2,1)S(1)}, bf16[512,128]{1,0:T(8,128)(2,1)S(1)}, ...), branch_computations={%region_0.0_spmd, %region_1.0_spmd, %region_2.0_spmd} | conditional | flops 6442450944 | bytes 25165832 | solution.py:445
  5.1 58.0 %branch_1_fun.2 = (bf16[32,64,1024]{2,1,0:T(8,128)(2,1)S(1)}, bf16[2,512,512]{2,1,0:T(8,128)(2,1)S(1)}) custom-call(bf16[2,512,1024]{2,1,0:T(8,128)(2,1)S(1)} %get-tuple-element.32.xs, bf16[512,128]{1,0:T(8,128)(2,1)S(1)} %get-tuple-element.33.cand, f32[8,128]{1,0:T(8,128)S(1)} %get-tuple-element.34.scale_ref), custom_call_target="tpu_custom_call" | custom-call | flops 3221225472 | bytes 8388608 | tf_op jit(solution)/shard_map/cond/branch_1_fun/pallas_call | solution.py:380
  63.1 4.5 %branch_1_fun.3 = f32[64,1,32,1024]{3,2,1,0:T(8,128)S(1)} custom-call(bf16[32,64,1024]{2,1,0:T(8,128)(2,1)S(1)} %get-tuple-element.35.cross_ref, bf16[2,512,512]{2,1,0:T(8,128)(2,1)S(1)} %get-tuple-element.36.weights_ref), custom_call_target="tpu_custom_call" | custom-call | flops 2147483648 | bytes 16777216 | tf_op jit(solution)/shard_map/cond/branch_1_fun/pallas_call | solution.py:424
  68.1 0.0 copy-start.2
  68.1 3.4 %copy-done.2 = f32[64,1,32,1024]{3,2,1,0:T(8,128)} copy-done((f32[64,1,32,1024]{3,2,1,0:T(8,128)}, f32[64,1,32,1024]{3,2,1,0:T(8,128)S(1)}, u32[]{:S(2)}) %copy-start.2) | copy-done | bytes 8388632
Async XLA Ops:
  0.7 1.5 %copy-start = (bf16[2,30,16,1024]{3,2,1,0:T(8,128)(2,1)S(1)}, bf16[2,30,16,1024]{3,2,1,0:T(8,128)(2,1)}, u32[]{:S(2)}) copy-start(bf16[2,30,16,1024]{3,2,1,0:T(8,128)(2,1)} %x_ref.1) | copy-start | bytes 5898244
  2.2 0.7 copy-start.1
  68.1 3.4 %copy-start.2 = (f32[64,1,32,1024]{3,2,1,0:T(8,128)}, f32[64,1,32,1024]{3,2,1,0:T(8,128)S(1)}, u32[]{:S(2)}) copy-start(f32[64,1,32,1024]{3,2,1,0:T(8,128)S(1)} %get-tuple-element.54) | copy-start | bytes 25165828

commit v6 on v5

--- a/solution.py
+++ b/solution.py
@@ -36,7 +36,7 @@
     return cos_part.astype(jnp.bfloat16), sin_part.astype(jnp.bfloat16)
 
 
-def pack_kernel(chans, band_ref, block_ref, flags_ref, x_ref, xs_ref, cand_ref, scale_ref, tier_ref, following):
+def pack_kernel(chans, band_ref, block_ref, flags_ref, x_ref, xs_ref, cand_ref, scale_ref, tier_ref, following, sems):
     depth = BINS * SLOTS
     f32, bf16 = jnp.float32, jnp.bfloat16
 
@@ -49,16 +49,26 @@
 
     valid = lax.fori_loop(0, SEG, link, 0)
 
+    def fetch(k, g):
+        place = pl.ds(pl.multiple_of(k * BINS, BINS), BINS)
+        return [
+            pltpu.make_async_copy(x_ref.at[comp, g], xs_ref.at[comp, place, :], sems.at[comp, k]) for comp in range(2)
+        ]
+
     def pack(k, at):
-        g = jnp.minimum(at, SEG - 1)
-        place = pl.ds(pl.multiple_of(k * BINS, BINS), BINS)
-        xs_ref[0, place, :] = x_ref[0, g]
-        xs_ref[1, place, :] = x_ref[1, g]
+        for copy in fetch(k, jnp.minimum(at, SEG - 1)):
+            copy.start()
         return following[jnp.minimum(at + 1, SEG)]
+
+    def packed_slot(k, carry):
+        for copy in fetch(k, 0):
+            copy.wait()
+        return carry
 
     tier = jnp.maximum((valid + 7) // 8 - 2, 0)
     tier_ref[0] = tier
     lax.fori_loop(0, 8 * (tier + 2), pack, following[0])
+    lax.fori_loop(0, 8 * (tier + 2), packed_slot, 0)
 
     first = block_ref[0] * SRC
     width = RX * chans
@@ -136,6 +146,19 @@
 
     lax.fori_loop(1, bands, rs_start, 0)
 
+    def a2a_copy(dest, origin):
+        return pltpu.make_async_remote_copy(
+            src_ref=send.at[dest], dst_ref=recv.at[origin],
+            send_sem=a2a_send.at[dest], recv_sem=a2a_recv.at[origin],
+            device_id=(dest, b), device_id_type=MESH)
+
+    def a2a_start(i, carry):
+        a2a_copy(lax.rem(c + i, chans), c).start()
+        return carry
+
+    early = min(9, chans)
+    lax.fori_loop(1, early, a2a_start, 0)
+
     count = min(32, bins // 2)
 
     def fill(i, carry):
@@ -180,16 +203,6 @@
         return carry
 
     lax.fori_loop(0, half, ag_start, 0)
-
-    def a2a_copy(dest, origin):
-        return pltpu.make_async_remote_copy(
-            src_ref=send.at[dest], dst_ref=recv.at[origin],
-            send_sem=a2a_send.at[dest], recv_sem=a2a_recv.at[origin],
-            device_id=(dest, b), device_id_type=MESH)
-
-    def a2a_start(i, carry):
-        a2a_copy(lax.rem(c + i, chans), c).start()
-        return carry
 
     def ag_wait(start, number):
         def one(i, carry):
@@ -301,7 +314,7 @@
 
     for piece in range(pieces):
         begin(piece)
-    lax.fori_loop(1, chans, a2a_start, 0)
+    lax.fori_loop(early, chans, a2a_start, 0)
     for step in range(2, last + 2):
         for piece in range(pieces):
             advance(piece, step)
@@ -360,10 +373,10 @@
             jax.ShapeDtypeStruct((8, 128), jnp.float32),
             jax.ShapeDtypeStruct((1,), jnp.int32),
         ),
-        in_specs=[smem, smem, smem, vmem],
+        in_specs=[smem, smem, smem, pl.BlockSpec(memory_space=pltpu.HBM)],
         out_specs=(vmem, vmem, vmem, smem),
-        scratch_shapes=[pltpu.SMEM((SLOTS,), jnp.int32)],
-        compiler_params=pltpu.CompilerParams(vmem_limit_bytes=24 * 1024 * 1024),
+        scratch_shapes=[pltpu.SMEM((SLOTS,), jnp.int32), pltpu.SemaphoreType.DMA((2, SLOTS))],
+        compiler_params=pltpu.CompilerParams(vmem_limit_bytes=60 * 1024 * 1024),
     )(lax.axis_index("band").reshape(1), block, flags, x)
 
 

time: 71.6 us -> 59.4 us (0.83)
  Pallas kernels: 64 us -> 54.2 us
  local copies, waits for them, and re-layouts: 5.58 us -> 3.39 us
    pallas_call x1, Pallas kernels: 58 us -> 46.5 us  [stacked(): pl.pallas_call(functools.partial(stack_kernel, tiles, chans, bands), out_...]
    unnamed x6 -> x2, local copies, waits for them, and re-layouts: 5.58 us -> 3.39 us
    pallas_call x1, Pallas kernels: 1.5 us -> 3.18 us  [packed(): pl.pallas_call(functools.partial(pack_kernel, chans), out_shape=(jax.Shap...]
where the time goes in v6:
time: 59.4 us; the launch traced here: 59.2 us
  Pallas kernels  54.2 us (91%)
  local copies, waits for them, and re-layouts  3.39 us (6%)
  between operations  1.37 us (2%)
    pallas_call x1, Pallas kernels, stacked(): pl.pallas_call(functools.partial(stack_kernel, tiles, chans, bands), out_...  46.5 us
    pallas_call x1, Pallas kernels, correlate(): pl.pallas_call(lag_kernel, out_shape=jax.ShapeDtypeStruct((SRC, 1, RX, LA...  4.53 us
    unnamed x2, local copies, waits for them, and re-layouts  3.39 us
    pallas_call x1, Pallas kernels, packed(): pl.pallas_call(functools.partial(pack_kernel, chans), out_shape=(jax.Shap...  3.18 us

profile of v6, /device:TPU:1, one launch (start us, length us, event | category | flops | bytes accessed | tf_op | source)
XLA Modules:
  0.0 59.2 jit_solution(659174223749781390)
XLA Ops:
  0.7 3.2 %shard_map.40 = (bf16[2,512,1024]{2,1,0:T(8,128)(2,1)S(1)}, bf16[512,128]{1,0:T(8,128)(2,1)S(1)}, f32[8,128]{1,0:T(8,128)S(1)}, s32[1]{0:T(128)}) custom-call(s32[1]{0:T(128)} %bitcast.band_ref, s32[1]{0:T(128)S(6)} %copy.10.block_ref, s32[30]{0:T(128)} %flags_ref.1, bf16[2,30,16,1024]{3,2,1,0:T(8,128)(2,1)} %x_ref.1), custom_call_target="tpu_custom_call" | custom-call | tf_op jit(solution)/shard_map/pallas_call | solution.py:368
  4.5 51.2 %conditional.1 = (f32[64,1,32,1024]{3,2,1,0:T(8,128)S(1)}) conditional(s32[]{:T(128)} %bitcast.1, (bf16[2,512,1024]{2,1,0:T(8,128)(2,1)S(1)}, bf16[512,128]{1,0:T(8,128)(2,1)S(1)}, f32[8,128]{1,0:T(8,128)S(1)}) %tuple.14, (bf16[2,512,1024]{2,1,0:T(8,128)(2,1)S(1)}, bf16[512,128]{1,0:T(8,128)(2,1)S(1)}, ...), branch_computations={%region_0.0_spmd, %region_1.0_spmd, %region_2.0_spmd} | conditional | flops 6442450944 | bytes 25165832 | solution.py:458
  4.5 46.5 %branch_0_fun.2 = (bf16[32,64,1024]{2,1,0:T(8,128)(2,1)S(1)}, bf16[2,512,512]{2,1,0:T(8,128)(2,1)S(1)}) custom-call(bf16[2,512,1024]{2,1,0:T(8,128)(2,1)S(1)} %get-tuple-element.26.xs, bf16[512,128]{1,0:T(8,128)(2,1)S(1)} %get-tuple-element.28.cand, f32[8,128]{1,0:T(8,128)S(1)} %get-tuple-element.29.scale_ref), custom_call_target="tpu_custom_call" | custom-call | flops 2147483648 | bytes 8388608 | tf_op jit(solution)/shard_map/cond/branch_0_fun/pallas_call | solution.py:393
  51.0 4.5 %branch_0_fun.3 = f32[64,1,32,1024]{3,2,1,0:T(8,128)S(1)} custom-call(bf16[32,64,1024]{2,1,0:T(8,128)(2,1)S(1)} %get-tuple-element.30.cross_ref, bf16[2,512,512]{2,1,0:T(8,128)(2,1)S(1)} %get-tuple-element.31.weights_ref), custom_call_target="tpu_custom_call" | custom-call | flops 2147483648 | bytes 16777216 | tf_op jit(solution)/shard_map/cond/branch_0_fun/pallas_call | solution.py:437
  55.8 0.0 copy-start
  55.8 3.4 %copy-done = f32[64,1,32,1024]{3,2,1,0:T(8,128)} copy-done((f32[64,1,32,1024]{3,2,1,0:T(8,128)}, f32[64,1,32,1024]{3,2,1,0:T(8,128)S(1)}, u32[]{:S(2)}) %copy-start) | copy-done | bytes 8388632
Async XLA Ops:
  55.8 3.4 %copy-start = (f32[64,1,32,1024]{3,2,1,0:T(8,128)}, f32[64,1,32,1024]{3,2,1,0:T(8,128)S(1)}, u32[]{:S(2)}) copy-start(f32[64,1,32,1024]{3,2,1,0:T(8,128)S(1)} %get-tuple-element.54) | copy-start | bytes 25165828
